TPU v7x, 512 devices: a whole 4x8x8 slice. The times are simulated.
512 devices in a mesh: dp: 64 (over y_hi, z, core), mp: 8 (over y_lo, x).
Axes of the slice: x: 4, y: 8 (y_hi: 4, y_lo: 2; y = y_hi * 2 + y_lo), z: 8, core: 2. Of those that a mesh axis runs over, the one named last changes fastest.
Arguments:
- spec_feat: bfloat16 [8192, 2048], P('dp', 'mp'), may hold values from -6 to 6
- pep_feat: bfloat16 [8192, 2048], P('dp', 'mp'), may hold values from -6 to 6
- w_spec: bfloat16 [2048, 768], P('mp'), may hold values from -0.125 to 0.125
- w_pep: bfloat16 [2048, 768], P('mp'), may hold values from -0.125 to 0.125
- teach_spec: bfloat16 [8192, 768], P('dp'), may hold values from -6 to 6
- teach_pep: bfloat16 [8192, 768], P(('dp', 'mp')), may hold values from -6 to 6
- exp_spec: int32 [768], replicated, may hold values from 6 to 8
- exp_pep: int32 [768], replicated, may hold values from 6 to 8
- positive: int32 [8192], P('dp'), may hold values from 0 to 8191
Outputs:
- spec_grad: float32 [8192, 768], P(('dp', 'mp'))
- pep_grad: float32 [8192, 768], P(('dp', 'mp'))
All inputs are finite; a program needn't handle non-finite values.
Results may differ from a plain program's by a relative error of at most 0.0024.
Values may be sent and summed in bfloat16 or wider, within the bound.
No kernel may reach another device: no remote copies, remote signals or barrier semaphores. Data moves between devices by JAX's collectives and lax.ppermute only.
A program may use at most 64 MiB of HBM per device.

v0:
```python
import math

import jax
import jax.numpy as jnp
from jax import lax
from jax.sharding import PartitionSpec as P

LOGIT_GAIN = 4.0
LOGIT_SHIFT = -2.0
CLIP_LEVELS = 127.0


def clip_channels(pre_proj, exponents):
    limits = CLIP_LEVELS * jnp.exp2(-exponents.astype(jnp.float32))
    return jnp.clip(pre_proj, -limits, limits).astype(jnp.bfloat16)


def project_spectra(spec_feat, w_spec, exp_spec):
    partial_sums = jnp.dot(spec_feat, w_spec, preferred_element_type=jnp.float32)
    return clip_channels(lax.psum(partial_sums, "mp"), exp_spec)


def project_peptides(pep_feat, w_pep, exp_pep):
    partial_sums = jnp.dot(pep_feat, w_pep, preferred_element_type=jnp.float32)
    return clip_channels(
        lax.psum_scatter(partial_sums, "mp", scatter_dimension=0, tiled=True), exp_pep
    )


def body(spec_feat, pep_feat, w_spec, w_pep, teach_spec, teach_pep, exp_spec, exp_pep, positive):
    factor = LOGIT_GAIN / math.sqrt(w_spec.shape[1])
    spec_q = project_spectra(spec_feat, w_spec, exp_spec)
    pep_q = project_peptides(pep_feat, w_pep, exp_pep)
    mp_count = lax.axis_size("mp")
    mp_index = lax.axis_index("mp")
    pep_rows = pep_q.shape[0]
    inner = (((1,), (1,)), ((), ()))
    outer = (((0,), (0,)), ((), ()))
    pep_all, teach_all = (
        lax.all_gather(pep_q, "dp", axis=0, tiled=True),
        lax.all_gather(teach_pep, "dp", axis=0, tiled=True),
    )
    local_ids = jnp.arange(pep_all.shape[0], dtype=jnp.int32)
    global_ids = (local_ids // pep_rows * mp_count + mp_index) * pep_rows + local_ids % pep_rows
    student = (
        factor * lax.dot_general(pep_all, spec_q, inner, preferred_element_type=jnp.float32)
        + LOGIT_SHIFT
    )
    teacher = factor * lax.dot_general(
        teach_all, teach_spec, inner, preferred_element_type=jnp.float32
    )
    hard = (global_ids[:, None] == positive[None, :]).astype(jnp.float32)
    target = 0.5 * hard + 0.5 * jax.nn.sigmoid(teacher)
    grad_table = (jax.nn.sigmoid(student) - target).astype(jnp.bfloat16)
    spec_acc = lax.dot_general(grad_table, pep_all, outer, preferred_element_type=jnp.float32)
    pep_grad = factor * lax.psum_scatter(
        jnp.dot(grad_table, spec_q, preferred_element_type=jnp.float32),
        "dp",
        scatter_dimension=0,
        tiled=True,
    )
    spec_grad = factor * lax.psum_scatter(spec_acc, "mp", scatter_dimension=0, tiled=True)
    return (spec_grad, pep_grad)


def solution(mesh):
    in_specs = (
        P("dp", "mp"),
        P("dp", "mp"),
        P("mp", None),
        P("mp", None),
        P("dp", None),
        P(("dp", "mp"), None),
        P(),
        P(),
        P("dp"),
    )
    out_specs = (P(("dp", "mp"), None), P(("dp", "mp"), None))
    return jax.shard_map(body, mesh=mesh, in_specs=in_specs, out_specs=out_specs, check_vma=False)
```

profile of v0, /device:TPU:1, one launch (start us, length us, event | category | flops | bytes accessed | tf_op | source)
XLA Modules:
  0.0 393.1 jit_solution(2753596625350133026)
XLA Ops:
  8.0 0.0 copy-start
  8.0 0.0 copy-start.2
  8.0 0.0 copy-start.3
  8.0 0.0 copy-start.5
  8.0 0.0 copy-start.4
  8.1 0.0 reduce-scatter.4.cloned.1.call-start
  8.1 0.9 copy-done
  9.0 1.8 fusion.27
  10.8 0.0 reduce-scatter.4.cloned.1.call-update
  10.8 0.0 all-gather.5.cloned.1.call-start
  10.9 0.5 all-gather.5.cloned.1.call-update
  11.4 0.0 all-gather.3.cloned.1.call-start
  11.5 0.7 exponential_multiply_fusion.1
  12.2 43.4 %reduce-scatter.4.cloned.1.call-done = f32[16,768]{1,0:T(8,128)} async-done(((f32[128,768]{1,0:T(8,128)}), f32[16,768]{1,0:T(8,128)}) %reduce-scatter.4.cloned.1.call-update) | async-done | bytes 49168 | tf_op jit(solution)/shard_map/reduce_scatter | solution.py:26
  55.5 1.4 minimum_convert_fusion.1
  56.9 0.0 all-gather.3.cloned.1.call-update
  57.0 0.0 reduce-scatter.6.cloned.1.call-start
  57.0 0.0 copy-done.2
  57.0 1.1 fusion.28
  58.1 0.0 copy-done.3
  58.1 32.0 %all-reduce.1 = bf16[128,768]{1,0:T(8,128)(2,1)S(1)} all-reduce(f32[128,768]{1,0:T(8,128)S(1)} %fusion.28), channel_id=1, replica_groups=mesh['dp'=64,'mp'=8] {'mp'}, use_global_device_ids=true, to_apply=%region_1.2 | all-reduce | flops 98304 | bytes 589824 | tf_op jit(solution)/shard_map/psum | solution.py:20
  90.1 14.8 %all-gather.5.cloned.1.call-done = bf16[1024,768]{1,0:T(8,128)(2,1)} async-done(((bf16[16,768]{1,0:T(8,128)(2,1)}), bf16[1024,768]{1,0:T(8,128)(2,1)}) %all-gather.5.cloned.1.call-update) | async-done | bytes 1572880 | tf_op jit(solution)/shard_map/all_gather | solution.py:41
  104.9 0.0 copy-done.5
  104.9 0.0 copy-done.4
  104.9 2.0 fusion.11
  106.9 82.5 %all-gather.3.cloned.1.call-done = bf16[1024,768]{1,0:T(8,128)(2,1)} async-done(((bf16[16,768]{1,0:T(8,128)(2,1)}), bf16[1024,768]{1,0:T(8,128)(2,1)}) %all-gather.3.cloned.1.call-update) | async-done | bytes 1572880 | tf_op jit(solution)/shard_map/all_gather | solution.py:40
  189.4 0.0 copy-start.1
  189.4 2.1 fusion.12
  191.6 0.0 copy-done.1
  191.6 1.2 fusion.29
  192.7 0.0 reduce-scatter.6.cloned.1.call-update
  192.8 0.0 reduce-scatter.8.cloned.1.call-start
  192.8 2.2 fusion.13
  195.0 0.0 reduce-scatter.8.cloned.1.call-update
  195.0 31.7 %reduce-scatter.6.cloned.1.call-done = f32[16,768]{1,0:T(8,128)} async-done(((f32[128,768]{1,0:T(8,128)}), f32[16,768]{1,0:T(8,128)}) %reduce-scatter.6.cloned.1.call-update) | async-done | bytes 49168 | tf_op jit(solution)/shard_map/reduce_scatter | solution.py:62
  226.7 1.4 broadcast_multiply_fusion.1
  228.1 156.4 %reduce-scatter.8.cloned.1.call-done = f32[16,768]{1,0:T(8,128)} async-done(((f32[1024,768]{1,0:T(8,128)}), f32[16,768]{1,0:T(8,128)}) %reduce-scatter.8.cloned.1.call-update) | async-done | bytes 49168 | tf_op jit(solution)/shard_map/reduce_scatter | solution.py:56
  384.5 1.4 broadcast_multiply_fusion
  (2 shorter events, 0.0 us)
Async XLA Ops:
  8.0 1.0 copy-start
  8.0 49.0 %copy-start.2 = (bf16[256,768]{1,0:T(8,128)(2,1)S(1)}, bf16[256,768]{1,0:T(8,128)(2,1)}, u32[]{:S(2)}) copy-start(bf16[256,768]{1,0:T(8,128)(2,1)} %param.11) | copy-start | bytes 1179652
  8.0 50.1 %copy-start.3 = (s32[768]{0:T(1024)S(1)}, s32[768]{0:T(1024)}, u32[]{:S(2)}) copy-start(s32[768]{0:T(1024)} %param.15) | copy-start | bytes 9220
  8.0 96.9 %copy-start.5 = (s32[128]{0:T(128)S(1)}, s32[128]{0:T(128)}, u32[]{:S(2)}) copy-start(s32[128]{0:T(128)} %param.17) | copy-start | bytes 1540
  8.0 96.9 %copy-start.4 = (bf16[128,768]{1,0:T(8,128)(2,1)S(1)}, bf16[128,768]{1,0:T(8,128)(2,1)}, u32[]{:S(2)}) copy-start(bf16[128,768]{1,0:T(8,128)(2,1)} %param.13) | copy-start | bytes 589828
  8.1 47.5 %reduce-scatter.4.cloned.1.call-start = ((), (), s32[]{:S(2)}) async-start(), calls=%async_computation.3 | async-start | bytes 442368 | tf_op jit(solution)/shard_map/reduce_scatter | solution.py:26
  10.8 94.1 %all-gather.5.cloned.1.call-start = ((), (), s32[]{:S(2)}) async-start(), calls=%async_computation.5 | async-start | bytes 1597440 | tf_op jit(solution)/shard_map/all_gather | solution.py:41
  11.4 178.0 %all-gather.3.cloned.1.call-start = ((), (), s32[]{:S(2)}) async-start(), calls=%async_computation.4 | async-start | bytes 1597440 | tf_op jit(solution)/shard_map/all_gather | solution.py:40
  57.0 169.7 %reduce-scatter.6.cloned.1.call-start = ((), (), s32[]{:S(2)}) async-start(), calls=%async_computation.6 | async-start | bytes 442368 | tf_op jit(solution)/shard_map/reduce_scatter | solution.py:62
  189.4 2.1 copy-start.1
  192.8 191.8 %reduce-scatter.8.cloned.1.call-start = ((), (), s32[]{:S(2)}) async-start(), calls=%async_computation.7 | async-start | bytes 3194880 | tf_op jit(solution)/shard_map/reduce_scatter | solution.py:56
Sparse Core Ops, SparseCore 0:
  11.7 43.7 reduce-scatter.3
  192.9 33.7 reduce-scatter.5
  231.4 153.0 reduce-scatter.7
Sparse Core Ops, SparseCore 1:
  15.2 89.7 all-gather.4
  109.2 80.2 all-gather.2
where the time goes:
time: 397 us; the launch traced here: 393 us
  waiting for transfers between devices  329 us (83%)
  blocking collectives  32 us (8%)
  between operations  15.3 us (4%)
  matrix products  10.3 us (3%)
  other arithmetic  4.98 us (1%)
    reduce_scatter x1, waiting for transfers between devices, body(): lax.psum_scatter(jnp.dot(grad_table, spec_q, preferred_element_type=jnp.f...  156 us
    all_gather x1, waiting for transfers between devices, body(): lax.all_gather(pep_q, 'dp', axis=0, tiled=True)  82.5 us
    reduce_scatter x1, waiting for transfers between devices, project_peptides(): lax.psum_scatter(partial_sums, 'mp', scatter_dimension=0, tiled=True)  43.4 us
    psum x1, blocking collectives, project_spectra(): return clip_channels(lax.psum(partial_sums, 'mp'), exp_spec)  32 us
    reduce_scatter x1, waiting for transfers between devices, body(): lax.psum_scatter(spec_acc, 'mp', scatter_dimension=0, tiled=True)  31.7 us
    all_gather x1, waiting for transfers between devices, body(): lax.all_gather(teach_pep, 'dp', axis=0, tiled=True)  14.8 us
  transfers between devices with their start and end apart: 5, of which 5 were waited for; matrix products, arithmetic and copies ran while one was open for 2% of the time, Pallas kernels for 0%

commit v1 on v0

v1 whole, which is shorter than its diff:
```python
import math

import numpy as np

import jax
import jax.numpy as jnp
from jax import lax
from jax.sharding import PartitionSpec as P

LOGIT_GAIN = 4.0
LOGIT_SHIFT = -2.0
CLIP_LEVELS = 127.0
AXES = ("dp", "mp")


def device_groups(mesh):
    flat = np.arange(mesh.shape["dp"] * mesh.shape["mp"]).reshape(4, 8, 2, 2, 2, 2)
    core_mp = flat.transpose(0, 1, 2, 3, 4, 5).reshape(32, 16)
    even = flat[:, :, 0]
    odd = flat[:, :, 1]
    spec_side = even.transpose(1, 3, 0, 2, 4).reshape(16, 16)
    pep_side = odd.transpose(0, 2, 4, 1, 3).reshape(16, 16)
    grid = np.concatenate([spec_side, pep_side], 0)
    pairs = [(int(a), int(b)) for a, b in zip(flat[:, :, 0].ravel(), flat[:, :, 1].ravel())]
    swap = pairs + [(b, a) for a, b in pairs]
    return core_mp.tolist(), grid.tolist(), swap


def body(groups, spec_feat, pep_feat, w_spec, w_pep, teach_spec, teach_pep, exp_spec, exp_pep, positive):
    core_mp, grid, swap = groups
    width = w_spec.shape[1]
    factor = LOGIT_GAIN / math.sqrt(width)
    rows = teach_pep.shape[0]
    dp_index = lax.axis_index("dp")
    mp_index = lax.axis_index("mp")
    even = dp_index % 2 == 0

    tags_spec = lax.dynamic_slice_in_dim(positive, mp_index * rows, rows)
    tags_pep = (dp_index * 8 + mp_index) * rows + jnp.arange(rows, dtype=jnp.int32)

    def with_tags(teach, tags):
        hi = (tags // 128).astype(jnp.bfloat16)[:, None]
        lo = (tags % 128).astype(jnp.bfloat16)[:, None]
        return jnp.concatenate([teach, hi, lo, jnp.zeros((rows, 126), jnp.bfloat16)], 1)

    t_spec = with_tags(lax.dynamic_slice_in_dim(teach_spec, mp_index * rows, rows), tags_spec)
    t_pep = with_tags(teach_pep, tags_pep)
    keep = jnp.where(even, t_spec, t_pep)
    got = lax.ppermute(jnp.where(even, t_pep, t_spec), AXES, swap)
    teach_rows = jnp.concatenate([jnp.where(even, keep, got), jnp.where(even, got, keep)], 0)

    part_spec = jnp.dot(spec_feat, w_spec, preferred_element_type=jnp.float32).astype(jnp.float16)
    part_pep = jnp.dot(pep_feat, w_pep, preferred_element_type=jnp.float32).astype(jnp.float16)
    parts = jnp.concatenate([part_spec.reshape(8, rows, width), part_pep.reshape(8, rows, width)], 0)
    parts = lax.all_to_all(parts, AXES, 0, 0, axis_index_groups=core_mp)
    sums = parts.reshape(2, 8, rows, width).astype(jnp.float32).sum(1).reshape(2 * rows, width)
    limits = CLIP_LEVELS * jnp.exp2(-jnp.where(even, exp_spec, exp_pep).astype(jnp.float32))
    q_rows = jnp.clip(sums, -limits, limits).astype(jnp.bfloat16)

    mine = jnp.concatenate([q_rows, teach_rows], 1)
    mine = lax.all_to_all(
        jnp.broadcast_to(mine[None], (16,) + mine.shape), AXES, 0, 0, axis_index_groups=grid
    ).reshape(16 * 2 * rows, -1)
    other = lax.ppermute(mine, AXES, swap)

    def unpack(block):
        tags = block[:, 2 * width : 2 * width + 2].astype(jnp.float32)
        return block[:, :width], block[:, width : 2 * width], 128.0 * tags[:, 0] + tags[:, 1]

    q_mine, t_mine, tag_mine = unpack(mine)
    q_other, t_other, tag_other = unpack(other)
    inner = (((1,), (1,)), ((), ()))
    student = factor * lax.dot_general(q_mine, q_other, inner, preferred_element_type=jnp.float32) + LOGIT_SHIFT
    teacher = factor * lax.dot_general(t_mine, t_other, inner, preferred_element_type=jnp.float32)
    hard = (tag_mine[:, None] == tag_other[None, :]).astype(jnp.float32)
    target = 0.5 * hard + 0.5 * jax.nn.sigmoid(teacher)
    grads = (jax.nn.sigmoid(student) - target).astype(jnp.bfloat16)
    acc = jnp.dot(grads, q_other, preferred_element_type=jnp.float32).astype(jnp.float16)
    acc = lax.all_to_all(acc.reshape(16, 2 * rows, width), AXES, 0, 0, axis_index_groups=grid)
    acc = factor * acc.astype(jnp.float32).sum(0)
    first, second = acc[:rows], acc[rows:]
    own = jnp.where(even, first, second)
    swapped = lax.ppermute(jnp.where(even, second, first), AXES, swap)
    return jnp.where(even, own, swapped), jnp.where(even, swapped, own)


def solution(mesh):
    groups = device_groups(mesh)

    def run(*args):
        return body(groups, *args)

    in_specs = (
        P("dp", "mp"),
        P("dp", "mp"),
        P("mp", None),
        P("mp", None),
        P("dp", None),
        P(("dp", "mp"), None),
        P(),
        P(),
        P("dp"),
    )
    out_specs = (P(("dp", "mp"), None), P(("dp", "mp"), None))
    return jax.shard_map(run, mesh=mesh, in_specs=in_specs, out_specs=out_specs, check_vma=False)
```

time: 397 us -> 97 us (0.24)
  waiting for transfers between devices: 329 us -> 10.2 us
  blocking collectives: 32 us -> 56.8 us
  starting transfers between devices: 0.21 us -> 16.2 us
  between operations: 15.3 us -> 0.81 us
    reduce_scatter x3 -> x0, waiting for transfers between devices: 231 us -> none  [the longest x1 156 us: body(): lax.psum_scatter(jnp.dot(grad_table, spec_q, preferred_element_type=jnp.f...]
    all_gather x2 -> x0, waiting for transfers between devices: 97.3 us -> none  [the longest x1 82.5 us: body(): lax.all_gather(pep_q, 'dp', axis=0, tiled=True)]
    all_to_all x0 -> x2, blocking collectives: none -> 56.8 us  [the longest x1 33.3 us: body(): lax.all_to_all(jnp.broadcast_to(mine[None], (16,) + mine.shape), AXES, 0,...]
    psum x1 -> x0, blocking collectives: 32 us -> none  [project_spectra(): return clip_channels(lax.psum(partial_sums, 'mp'), exp_spec)]
    all_to_all x0 -> x1, starting transfers between devices: none -> 10.3 us  [body(): parts = lax.all_to_all(parts, AXES, 0, 0, axis_index_groups=core_mp)]
    ppermute x0 -> x3, starting transfers between devices: none -> 5.92 us  [the longest x1 2.09 us: body(): got = lax.ppermute(jnp.where(even, t_pep, t_spec), AXES, swap)]
    ppermute x0 -> x3, waiting for transfers between devices: none -> 5.45 us  [the longest x1 3.3 us: body(): other = lax.ppermute(mine, AXES, swap)]
    all_to_all x0 -> x1, waiting for transfers between devices: none -> 4.75 us  [body(): parts = lax.all_to_all(parts, AXES, 0, 0, axis_index_groups=core_mp)]
  transfers between devices with their start and end apart: 5 -> 4, of which waited for: 5 -> 4; matrix products, arithmetic and copies ran while one was open for 2% -> 2% of each run, Pallas kernels for 0% -> 0%
where the time goes in v1:
time: 97 us; the launch traced here: 96.5 us
  blocking collectives  56.8 us (59%)
  starting transfers between devices  16.2 us (17%)
  waiting for transfers between devices  10.2 us (11%)
  matrix products  7 us (7%)
  local copies, waits for them, and re-layouts  3.07 us (3%)
  other arithmetic  2.49 us (3%)
    all_to_all x1, blocking collectives, body(): lax.all_to_all(jnp.broadcast_to(mine[None], (16,) + mine.shape), AXES, 0,...  33.3 us
    all_to_all x1, blocking collectives, body(): lax.all_to_all(acc.reshape(16, 2 * rows, width), AXES, 0, 0, axis_index_g...  23.4 us
    all_to_all x1, starting transfers between devices, body(): parts = lax.all_to_all(parts, AXES, 0, 0, axis_index_groups=core_mp)  10.3 us
    all_to_all x1, waiting for transfers between devices, body(): parts = lax.all_to_all(parts, AXES, 0, 0, axis_index_groups=core_mp)  4.75 us
    ppermute x1, waiting for transfers between devices, body(): other = lax.ppermute(mine, AXES, swap)  3.3 us
    dot_general x1, matrix products, body(): jnp.dot(grads, q_other, preferred_element_type=jnp.float32)  2.93 us
    ppermute x1, starting transfers between devices, body(): got = lax.ppermute(jnp.where(even, t_pep, t_spec), AXES, swap)  2.09 us
  transfers between devices with their start and end apart: 4, of which 4 were waited for; matrix products, arithmetic and copies ran while one was open for 2% of the time, Pallas kernels for 0%

profile of v1, /device:TPU:1, one launch (start us, length us, event | category | flops | bytes accessed | tf_op | source)
XLA Modules:
  0.0 96.5 jit_solution(17540645277071262846)
XLA Ops:
  0.6 0.0 copy-start
  0.6 0.0 copy-start.5
  0.7 0.0 copy-start.1
  0.7 0.0 copy-start.4
  0.7 1.0 copy-done
  1.6 0.0 copy-start.3
  1.6 1.1 %convolution_convert_fusion.2 = f16[128,768]{1,0:T(8,128)(2,1)S(1)} fusion(bf16[128,256]{1,0:T(8,128)(2,1)} %param.9, bf16[256,768]{1,0:T(8,128)(2,1)S(1)} %copy-done), kind=kOutput, calls=%fused_computation.18 | convolution fusion | flops 50429952 | bytes 655360 | tf_op jit(solution)/shard_map/dot_general | solution.py:52
  2.7 1.3 %convolution_convert_fusion.1 = f16[128,768]{1,0:T(8,128)(2,1)S(1)} fusion(bf16[128,256]{1,0:T(8,128)(2,1)} %param.10, bf16[256,768]{1,0:T(8,128)(2,1)} %param.12), kind=kOutput, calls=%fused_computation.17 | convolution fusion | flops 50429952 | bytes 655360 | tf_op jit(solution)/shard_map/dot_general | solution.py:53
  4.0 0.8 pad_maximum_fusion
  4.8 10.3 %all-to-all-start = ((f16[16,16,768]{2,1,0:T(8,128)(2,1)}), f16[16,16,768]{2,1,0:T(8,128)(2,1)S(1)}, u32[]{:S(2)}, u32[]{:S(2)}) async-start(f16[16,16,768]{2,1,0:T(8,128)(2,1)} %pad_maximum_fusion), calls=%async_computation | async-start | bytes 786432 | tf_op jit(solution)/shard_map/all_to_all | solution.py:55
  15.1 0.0 copy-done.5
  15.1 0.1 convert_bitcast_fusion
  15.2 0.1 copy.17
  15.3 0.1 copy.16
  15.4 0.7 constant_dynamic-slice_fusion
  16.1 0.1 pad.10.clone
  16.2 0.0 copy-done.1
  16.2 0.1 broadcast_select_fusion.2
  16.3 2.1 %collective-permute-start = (bf16[16,896]{1,0:T(8,128)(2,1)S(1)}, bf16[16,896]{1,0:T(8,128)(2,1)S(1)}, u32[]{:S(2)}, u32[]{:S(2)}) collective-permute-start(bf16[16,896]{1,0:T(8,128)(2,1)S(1)} %broadcast_select_fusion.2), channel_id=1, source_target_pairs={{0,8},{1,9},{2,10},{3,11},{4,12},{5,13},{6,14},{7,15},{16,24},{17,... | collective-permute-start | bytes 86024 | tf_op jit(solution)/shard_map/ppermute | solution.py:49
  18.4 0.0 copy-done.4
  18.4 0.0 copy-done.3
  18.4 0.9 collective-permute-done
  19.4 0.1 broadcast_select_fusion.1
  19.5 4.8 %all-to-all-done = f16[16,16,768]{2,1,0:T(8,128)(2,1)S(1)} async-done(((f16[16,16,768]{2,1,0:T(8,128)(2,1)}), f16[16,16,768]{2,1,0:T(8,128)(2,1)S(1)}, u32[]{:S(2)}, u32[]{:S(2)}) %all-to-all-start) | async-done | bytes 393248 | tf_op jit(solution)/shard_map/all_to_all | solution.py:55
  24.2 0.1 convert_reduce_fusion.1
  24.3 0.1 broadcast_in_dim.12
  24.5 33.3 %all_to_all.15 = bf16[16,32,1664]{2,1,0:T(8,128)(2,1)S(1)} all-to-all(bf16[16,32,1664]{2,1,0:T(8,128)(2,1)S(1)} %broadcast_in_dim.12), channel_id=1, replica_groups={{0,1,4,5,128,129,132,133,256,257,260,261,384,385,388,389},{2,3,6,7,130,..., dimensions={0} | all-to-all | bytes 3407872 | tf_op jit(solution)/shard_map/all_to_all | solution.py:61
  57.8 1.9 %collective-permute-start.1 = (bf16[512,1664]{1,0:T(8,128)(2,1)S(1)}, bf16[512,1664]{1,0:T(8,128)(2,1)S(1)}, u32[]{:S(2)}, u32[]{:S(2)}) collective-permute-start(bf16[512,1664]{1,0:T(8,128)(2,1)S(1)} %bitcast.21), channel_id=1, source_target_pairs={{0,8},{1,9},{2,10},{3,11},{4,12},{5,13},{6,14},{7,15},{16,24},{17,... | collective-permute-start | bytes 5111816 | tf_op jit(solution)/shard_map/ppermute | solution.py:64
  59.7 0.2 fusion.23
  60.0 3.3 %collective-permute-done.1 = bf16[512,1664]{1,0:T(8,128)(2,1)S(1)} collective-permute-done((bf16[512,1664]{1,0:T(8,128)(2,1)S(1)}, bf16[512,1664]{1,0:T(8,128)(2,1)S(1)}, u32[]{:S(2)}, u32[]{:S(2)}) %collective-permute-start.1) | collective-permute-done | bytes 1703968 | tf_op jit(solution)/shard_map/ppermute | solution.py:64
  63.3 0.0 copy-start.2
  63.3 0.2 fusion.22
  63.5 1.0 copy-done.2
  64.5 1.8 %fusion.10 = f32[512,512]{1,0:T(8,128)} fusion(bf16[512,1664]{1,0:T(8,128)(2,1)S(1)} %collective-permute-done.1, bf16[512,1664]{1,0:T(8,128)(2,1)S(1)} %bitcast.23, f32[512]{0:T(512)S(1)} %fusion.22, f32[512]{0:T(512)S(1)} %fusion.23), kind=kOutput, calls=%fused_computation.14 | convolution fusion | flops 404750336 | bytes 2625536 | tf_op jit(solution)/shard_map/dot_general | solution.py:74
  66.2 2.9 %convolution_convert_fusion = f16[512,768]{1,0:T(8,128)(2,1)S(1)} fusion(f32[512,512]{1,0:T(8,128)} %fusion.10, bf16[512,1664]{1,0:T(8,128)(2,1)} %copy-done.2, bf16[512,1664]{1,0:T(8,128)(2,1)S(1)} %bitcast.24), kind=kOutput, calls=%fused_computation.1 | convolution fusion | flops 807534592 | bytes 4194304 | tf_op jit(solution)/shard_map/dot_general | solution.py:78
  69.2 23.4 %all_to_all.16 = f16[16,32,768]{2,1,0:T(8,128)(2,1)S(1)} all-to-all(f16[16,32,768]{2,1,0:T(8,128)(2,1)S(1)} %bitcast.25), channel_id=1, replica_groups={{0,1,4,5,128,129,132,133,256,257,260,261,384,385,388,389},{2,3,6,7,130,..., dimensions={0} | all-to-all | bytes 1572864 | tf_op jit(solution)/shard_map/all_to_all | solution.py:79
  92.6 0.1 convert_reduce_fusion
  92.7 1.9 %collective-permute-start.2 = (f32[16,768]{1,0:T(8,128)S(1)}, f32[16,768]{1,0:T(8,128)S(1)}, u32[]{:S(2)}, u32[]{:S(2)}) collective-permute-start(f32[16,768]{1,0:T(8,128)S(1)} %slice_select_fusion), channel_id=1, source_target_pairs={{0,8},{1,9},{2,10},{3,11},{4,12},{5,13},{6,14},{7,15},{16,24},{17,... | collective-permute-start | bytes 147464 | tf_op jit(solution)/shard_map/ppermute | solution.py:83
  94.7 1.2 %collective-permute-done.2 = f32[16,768]{1,0:T(8,128)S(1)} collective-permute-done((f32[16,768]{1,0:T(8,128)S(1)}, f32[16,768]{1,0:T(8,128)S(1)}, u32[]{:S(2)}, u32[]{:S(2)}) %collective-permute-start.2) | collective-permute-done | bytes 49184 | tf_op jit(solution)/shard_map/ppermute | solution.py:83
  95.9 0.6 broadcast_select_fusion.4
  (10 shorter events, 0.1 us)
Async XLA Ops:
  0.6 1.0 %copy-start = (bf16[256,768]{1,0:T(8,128)(2,1)S(1)}, bf16[256,768]{1,0:T(8,128)(2,1)}, u32[]{:S(2)}) copy-start(bf16[256,768]{1,0:T(8,128)(2,1)} %param.11) | copy-start | bytes 1179652
  0.6 14.4 %copy-start.5 = (s32[128]{0:T(128)S(1)}, s32[128]{0:T(128)}, u32[]{:S(2)}) copy-start(s32[128]{0:T(128)} %param.17) | copy-start | bytes 1540
  0.7 15.6 %copy-start.1 = (bf16[16,768]{1,0:T(8,128)(2,1)S(1)}, bf16[16,768]{1,0:T(8,128)(2,1)}, u32[]{:S(2)}) copy-start(bf16[16,768]{1,0:T(8,128)(2,1)} %param.14) | copy-start | bytes 73732
  0.7 17.7 %copy-start.4 = (s32[768]{0:T(1024)S(1)}, s32[768]{0:T(1024)}, u32[]{:S(2)}) copy-start(s32[768]{0:T(1024)} %param.16) | copy-start | bytes 9220
  1.6 16.8 %copy-start.3 = (s32[768]{0:T(1024)S(1)}, s32[768]{0:T(1024)}, u32[]{:S(2)}) copy-start(s32[768]{0:T(1024)} %param.15) | copy-start | bytes 9220
  4.8 19.4 %all-to-all-start = ((f16[16,16,768]{2,1,0:T(8,128)(2,1)}), f16[16,16,768]{2,1,0:T(8,128)(2,1)S(1)}, u32[]{:S(2)}, u32[]{:S(2)}) async-start(f16[16,16,768]{2,1,0:T(8,128)(2,1)} %pad_maximum_fusion), calls=%async_computation | async-start | bytes 786432 | tf_op jit(solution)/shard_map/all_to_all | solution.py:55
  16.3 3.1 %collective-permute-start = (bf16[16,896]{1,0:T(8,128)(2,1)S(1)}, bf16[16,896]{1,0:T(8,128)(2,1)S(1)}, u32[]{:S(2)}, u32[]{:S(2)}) collective-permute-start(bf16[16,896]{1,0:T(8,128)(2,1)S(1)} %broadcast_select_fusion.2), channel_id=1, source_target_pairs={{0,8},{1,9},{2,10},{3,11},{4,12},{5,13},{6,14},{7,15},{16,24},{17,... | collective-permute-start | bytes 86024 | tf_op jit(solution)/shard_map/ppermute | solution.py:49
  57.8 5.5 %collective-permute-start.1 = (bf16[512,1664]{1,0:T(8,128)(2,1)S(1)}, bf16[512,1664]{1,0:T(8,128)(2,1)S(1)}, u32[]{:S(2)}, u32[]{:S(2)}) collective-permute-start(bf16[512,1664]{1,0:T(8,128)(2,1)S(1)} %bitcast.21), channel_id=1, source_target_pairs={{0,8},{1,9},{2,10},{3,11},{4,12},{5,13},{6,14},{7,15},{16,24},{17,... | collective-permute-start | bytes 5111816 | tf_op jit(solution)/shard_map/ppermute | solution.py:64
  63.3 1.2 %copy-start.2 = (bf16[512,1664]{1,0:T(8,128)(2,1)}, bf16[512,1664]{1,0:T(8,128)(2,1)S(1)}, u32[]{:S(2)}) copy-start(bf16[512,1664]{1,0:T(8,128)(2,1)S(1)} %collective-permute-done.1) | copy-start | bytes 5111812
  92.7 3.1 %collective-permute-start.2 = (f32[16,768]{1,0:T(8,128)S(1)}, f32[16,768]{1,0:T(8,128)S(1)}, u32[]{:S(2)}, u32[]{:S(2)}) collective-permute-start(f32[16,768]{1,0:T(8,128)S(1)} %slice_select_fusion), channel_id=1, source_target_pairs={{0,8},{1,9},{2,10},{3,11},{4,12},{5,13},{6,14},{7,15},{16,24},{17,... | collective-permute-start | bytes 147464 | tf_op jit(solution)/shard_map/ppermute | solution.py:83

commit v2 on v1

v2 whole, which is shorter than its diff:
```python
import math

import numpy as np

import jax
import jax.numpy as jnp
from jax import lax
from jax.experimental import pallas as pl
from jax.experimental.pallas import tpu as pltpu
from jax.sharding import PartitionSpec as P

LOGIT_GAIN = 4.0
LOGIT_SHIFT = -2.0
CLIP_LEVELS = 127.0
AXES = ("dp", "mp")


def pair_kernel(factor, width, mine, other, out, held, sems):
    ahead = [
        pltpu.make_async_copy(other.at[:, cols], held.at[:, cols], sems.at[i])
        for i, cols in enumerate((pl.ds(width, width + 128), pl.ds(0, width)))
    ]
    for copy in ahead:
        copy.start()
    inner = (((1,), (1,)), ((), ()))
    size = mine.shape[0] // 2
    lane = lax.broadcasted_iota(jnp.int32, (8, 128), 1)
    weigh = jnp.where(lane == 0, 128.0, jnp.where(lane == 1, 1.0, 0.0)).astype(jnp.bfloat16)
    ahead[0].wait()
    tag_other = lax.dot_general(weigh, held[:, 2 * width :], inner, preferred_element_type=jnp.float32)[0:1]
    targets = []
    for start in (0, size):
        at = pl.ds(start, size)
        teacher = lax.dot_general(
            mine[at, width : 2 * width], held[:, width : 2 * width], inner, preferred_element_type=jnp.float32
        )
        tags = mine[at, 2 * width :].astype(jnp.float32)
        tag_mine = 128.0 * tags[:, 0:1] + tags[:, 1:2]
        hard = jnp.where(tag_mine == tag_other, 0.5, 0.0)
        targets.append(0.25 * jnp.tanh((0.5 * factor) * teacher) - 0.25 + hard)
    ahead[1].wait()
    for start, target in zip((0, size), targets):
        at = pl.ds(start, size)
        student = lax.dot_general(mine[at, :width], held[:, :width], inner, preferred_element_type=jnp.float32)
        grads = 0.5 * jnp.tanh((0.5 * factor) * student + 0.5 * LOGIT_SHIFT) - target
        out[at, :] = jnp.dot(grads.astype(jnp.bfloat16), held[:, :width], preferred_element_type=jnp.float32)


def pair_grads(mine, other, factor, width):
    return pl.pallas_call(
        lambda *refs: pair_kernel(factor, width, *refs),
        out_shape=jax.ShapeDtypeStruct((mine.shape[0], width), jnp.float32),
        in_specs=[pl.BlockSpec(memory_space=pltpu.VMEM), pl.BlockSpec(memory_space=pl.ANY)],
        out_specs=pl.BlockSpec(memory_space=pltpu.VMEM),
        scratch_shapes=[pltpu.VMEM(other.shape, other.dtype), pltpu.SemaphoreType.DMA((2,))],
        compiler_params=pltpu.CompilerParams(vmem_limit_bytes=32 * 2**20),
    )(mine, other)


def device_groups(mesh):
    flat = np.arange(mesh.shape["dp"] * mesh.shape["mp"]).reshape(4, 8, 2, 2, 4)
    core_mp = flat.reshape(32, 16)
    flat = flat[..., [0, 1, 3, 2]].reshape(4, 8, 2, 2, 2, 2)
    even = flat[:, :, 0]
    odd = flat[:, :, 1]
    spec_side = even.transpose(1, 3, 0, 2, 4).reshape(16, 16)
    pep_side = odd.transpose(0, 2, 4, 1, 3).reshape(16, 16)
    grid = np.concatenate([spec_side, pep_side], 0)
    pairs = [(int(a), int(b)) for a, b in zip(flat[:, :, 0].ravel(), flat[:, :, 1].ravel())]
    swap = pairs + [(b, a) for a, b in pairs]
    return core_mp.tolist(), grid.tolist(), [list(pair) for pair in pairs], swap


def body(groups, spec_feat, pep_feat, w_spec, w_pep, teach_spec, teach_pep, exp_spec, exp_pep, positive):
    core_mp, grid, pairs, swap = groups
    width = w_spec.shape[1]
    factor = LOGIT_GAIN / math.sqrt(width)
    rows = teach_pep.shape[0]
    dp_index = lax.axis_index("dp")
    mp_index = lax.axis_index("mp")
    even = dp_index % 2 == 0

    tags_spec = lax.dynamic_slice_in_dim(positive, mp_index * rows, rows)
    tags_pep = (dp_index * 8 + mp_index) * rows + jnp.arange(rows, dtype=jnp.int32)

    def with_tags(teach, tags):
        hi = (tags // 128).astype(jnp.bfloat16)[:, None]
        lo = (tags % 128).astype(jnp.bfloat16)[:, None]
        return jnp.concatenate([teach, hi, lo, jnp.zeros((rows, 126), jnp.bfloat16)], 1)

    t_spec = with_tags(lax.dynamic_slice_in_dim(teach_spec, mp_index * rows, rows), tags_spec)
    t_pep = with_tags(teach_pep, tags_pep)
    keep = jnp.where(even, t_spec, t_pep)
    got = lax.ppermute(jnp.where(even, t_pep, t_spec), AXES, swap)
    teach_rows = jnp.concatenate([jnp.where(even, keep, got), jnp.where(even, got, keep)], 0)

    part_spec = jnp.dot(spec_feat, w_spec, preferred_element_type=jnp.float32)
    part_pep = jnp.dot(pep_feat, w_pep, preferred_element_type=jnp.float32)
    part_spec, part_pep = lax.optimization_barrier((part_spec, part_pep))
    parts = jnp.concatenate([part_spec.reshape(8, rows, width), part_pep.reshape(8, rows, width)], 0)
    parts = parts.astype(jnp.float16)
    parts = lax.all_to_all(parts, AXES, 0, 0, axis_index_groups=core_mp)
    sums = parts.reshape(2, 8, rows, width).astype(jnp.float32).sum(1).reshape(2 * rows, width)
    limits = CLIP_LEVELS * jnp.exp2(-jnp.where(even, exp_spec, exp_pep).astype(jnp.float32))
    q_rows = jnp.clip(sums, -limits, limits).astype(jnp.bfloat16)

    mine = jnp.concatenate([q_rows, teach_rows], 1)
    mine = lax.all_to_all(
        jnp.broadcast_to(mine[None], (16,) + mine.shape), AXES, 0, 0, axis_index_groups=grid
    ).reshape(16 * 2 * rows, -1)
    other = lax.ppermute(mine, AXES, swap)

    acc = pair_grads(mine, other, factor, width).astype(jnp.float16)
    acc = lax.all_to_all(acc.reshape(16, 2 * rows, width), AXES, 0, 0, axis_index_groups=grid)
    acc = factor * acc.astype(jnp.float32).sum(0)
    both = lax.all_gather(acc, AXES, axis=0, axis_index_groups=pairs).reshape(2, 2, rows, width)
    own = lax.dynamic_index_in_dim(both, dp_index % 2, 1, keepdims=False)
    return own[0], own[1]


def solution(mesh):
    groups = device_groups(mesh)

    def run(*args):
        return body(groups, *args)

    in_specs = (
        P("dp", "mp"),
        P("dp", "mp"),
        P("mp", None),
        P("mp", None),
        P("dp", None),
        P(("dp", "mp"), None),
        P(),
        P(),
        P("dp"),
    )
    out_specs = (P(("dp", "mp"), None), P(("dp", "mp"), None))
    return jax.shard_map(run, mesh=mesh, in_specs=in_specs, out_specs=out_specs, check_vma=False)
```

time: 97 us -> 92.2 us (0.951)
  blocking collectives: 56.8 us -> 35 us
  waiting for transfers between devices: 10.2 us -> 25.1 us
  starting transfers between devices: 16.2 us -> 21.2 us
  matrix products: 7 us -> 2.3 us
  Pallas kernels: 0 us -> 2.08 us
    all_to_all x1 -> x0, blocking collectives: 23.4 us -> none  [body(): lax.all_to_all(acc.reshape(16, 2 * rows, width), AXES, 0, 0, axis_index_g...]
    all_to_all x0 -> x1, waiting for transfers between devices: none -> 15.8 us  [body(): lax.all_to_all(acc.reshape(16, 2 * rows, width), AXES, 0, 0, axis_index_g...]
    all_to_all x0 -> x1, starting transfers between devices: none -> 6.9 us  [body(): lax.all_to_all(acc.reshape(16, 2 * rows, width), AXES, 0, 0, axis_index_g...]
    dot_general x4 -> x2, matrix products: 7 us -> 2.3 us  [the longest x1 1.25 us: body(): part_pep = jnp.dot(pep_feat, w_pep, preferred_element_type=jnp.float32)]
    pallas_call x0 -> x1, Pallas kernels: none -> 2.08 us  [pair_grads(): pl.pallas_call(lambda *refs: pair_kernel(factor, width, *refs), out_shape...]
    all_gather x0 -> x1, blocking collectives: none -> 1.95 us  [body(): lax.all_gather(acc, AXES, axis=0, axis_index_groups=pairs)]
    ppermute x1 -> x0, starting transfers between devices: 1.92 us -> none  [body(): swapped = lax.ppermute(jnp.where(even, second, first), AXES, swap)]
    ppermute x1 -> x0, waiting for transfers between devices: 1.2 us -> none  [body(): swapped = lax.ppermute(jnp.where(even, second, first), AXES, swap)]
  transfers between devices with their start and end apart: 4 -> 4, of which waited for: 4 -> 4; matrix products, arithmetic and copies ran while one was open for 2% -> 1% of each run, Pallas kernels for 0% -> 0%
where the time goes in v2:
time: 92.2 us; the launch traced here: 91.6 us
  blocking collectives  35 us (38%)
  waiting for transfers between devices  25.1 us (27%)
  starting transfers between devices  21.2 us (23%)
  local copies, waits for them, and re-layouts  2.8 us (3%)
  other arithmetic  2.34 us (3%)
  matrix products  2.3 us (2%)
  Pallas kernels  2.08 us (2%)
    all_to_all x1, blocking collectives, body(): lax.all_to_all(jnp.broadcast_to(mine[None], (16,) + mine.shape), AXES, 0,...  33 us
    all_to_all x1, waiting for transfers between devices, body(): lax.all_to_all(acc.reshape(16, 2 * rows, width), AXES, 0, 0, axis_index_g...  15.8 us
    all_to_all x1, starting transfers between devices, body(): parts = lax.all_to_all(parts, AXES, 0, 0, axis_index_groups=core_mp)  10.3 us
    all_to_all x1, starting transfers between devices, body(): lax.all_to_all(acc.reshape(16, 2 * rows, width), AXES, 0, 0, axis_index_g...  6.9 us
    all_to_all x1, waiting for transfers between devices, body(): parts = lax.all_to_all(parts, AXES, 0, 0, axis_index_groups=core_mp)  4.76 us
    ppermute x1, waiting for transfers between devices, body(): other = lax.ppermute(mine, AXES, swap)  3.56 us
    ppermute x1, starting transfers between devices, body(): got = lax.ppermute(jnp.where(even, t_pep, t_spec), AXES, swap)  2.09 us
    pallas_call x1, Pallas kernels, pair_grads(): pl.pallas_call(lambda *refs: pair_kernel(factor, width, *refs), out_shape...  2.08 us
  transfers between devices with their start and end apart: 4, of which 4 were waited for; matrix products, arithmetic and copies ran while one was open for 1% of the time, Pallas kernels for 0%

profile of v2, /device:TPU:1, one launch (start us, length us, event | category | flops | bytes accessed | tf_op | source)
XLA Modules:
  0.0 91.6 jit_solution(15815184016847957567)
XLA Ops:
  0.6 0.0 copy-start
  0.6 1.0 %copy-done = bf16[256,768]{1,0:T(8,128)(2,1)S(1)} copy-done((bf16[256,768]{1,0:T(8,128)(2,1)S(1)}, bf16[256,768]{1,0:T(8,128)(2,1)}, u32[]{:S(2)}) %copy-start) | copy-done | bytes 393240
  1.6 1.0 %fusion.12 = f32[128,768]{1,0:T(8,128)S(1)} fusion(bf16[128,256]{1,0:T(8,128)(2,1)} %param.9, bf16[256,768]{1,0:T(8,128)(2,1)S(1)} %copy-done), kind=kOutput, calls=%fused_computation.41 | convolution fusion | flops 50331648 | bytes 851968 | tf_op jit(solution)/shard_map/dot_general | solution.py:97
  2.7 0.0 copy-start.4
  2.7 0.0 copy-start.1
  2.7 1.3 %fusion.13 = f32[128,768]{1,0:T(8,128)S(1)} fusion(bf16[128,256]{1,0:T(8,128)(2,1)} %param.10, bf16[256,768]{1,0:T(8,128)(2,1)} %param.12), kind=kOutput, calls=%fused_computation.42 | convolution fusion | flops 50331648 | bytes 851968 | tf_op jit(solution)/shard_map/dot_general | solution.py:98
  4.0 0.0 copy-start.2
  4.0 0.0 copy-start.3
  4.1 0.8 pad_maximum_fusion
  4.9 10.3 %all-to-all-start = ((f16[16,16,768]{2,1,0:T(8,128)(2,1)}), f16[16,16,768]{2,1,0:T(8,128)(2,1)S(1)}, u32[]{:S(2)}, u32[]{:S(2)}) async-start(f16[16,16,768]{2,1,0:T(8,128)(2,1)} %pad_maximum_fusion), calls=%async_computation | async-start | bytes 786432 | tf_op jit(solution)/shard_map/all_to_all | solution.py:102
  15.2 0.0 copy-done.4
  15.2 0.1 convert_bitcast_fusion
  15.3 0.1 copy.12
  15.4 0.1 copy.11
  15.5 0.7 constant_dynamic-slice_fusion
  16.2 0.1 pad.10.clone
  16.3 0.0 copy-done.1
  16.3 0.1 broadcast_select_fusion.2
  16.4 2.1 %collective-permute-start = (bf16[16,896]{1,0:T(8,128)(2,1)S(1)}, bf16[16,896]{1,0:T(8,128)(2,1)S(1)}, u32[]{:S(2)}, u32[]{:S(2)}) collective-permute-start(bf16[16,896]{1,0:T(8,128)(2,1)S(1)} %broadcast_select_fusion.2), channel_id=1, source_target_pairs={{0,8},{1,9},{3,11},{2,10},{4,12},{5,13},{7,15},{6,14},{16,24},{17,... | collective-permute-start | bytes 86024 | tf_op jit(solution)/shard_map/ppermute | solution.py:94
  18.5 0.0 copy-done.2
  18.5 0.0 copy-done.3
  18.5 0.9 %collective-permute-done = bf16[16,896]{1,0:T(8,128)(2,1)S(1)} collective-permute-done((bf16[16,896]{1,0:T(8,128)(2,1)S(1)}, bf16[16,896]{1,0:T(8,128)(2,1)S(1)}, u32[]{:S(2)}, u32[]{:S(2)}) %collective-permute-start) | collective-permute-done | bytes 28704 | tf_op jit(solution)/shard_map/ppermute | solution.py:94
  19.5 0.1 broadcast_select_fusion.1
  19.6 4.8 %all-to-all-done = f16[16,16,768]{2,1,0:T(8,128)(2,1)S(1)} async-done(((f16[16,16,768]{2,1,0:T(8,128)(2,1)}), f16[16,16,768]{2,1,0:T(8,128)(2,1)S(1)}, u32[]{:S(2)}, u32[]{:S(2)}) %all-to-all-start) | async-done | bytes 393248 | tf_op jit(solution)/shard_map/all_to_all | solution.py:102
  24.3 0.1 convert_reduce_fusion.1
  24.4 0.1 broadcast_in_dim.20
  24.6 33.0 %all_to_all.15 = bf16[16,32,1664]{2,1,0:T(8,128)(2,1)S(1)} all-to-all(bf16[16,32,1664]{2,1,0:T(8,128)(2,1)S(1)} %broadcast_in_dim.20), channel_id=1, replica_groups={{0,1,4,5,128,129,132,133,256,257,260,261,384,385,388,389},{3,2,7,6,131,..., dimensions={0} | all-to-all | bytes 3407872 | tf_op jit(solution)/shard_map/all_to_all | solution.py:108
  57.6 1.9 %collective-permute-start.1 = (bf16[512,1664]{1,0:T(8,128)(2,1)S(1)}, bf16[512,1664]{1,0:T(8,128)(2,1)S(1)}, u32[]{:S(2)}, u32[]{:S(2)}) collective-permute-start(bf16[512,1664]{1,0:T(8,128)(2,1)S(1)} %bitcast.26), channel_id=1, source_target_pairs={{0,8},{1,9},{3,11},{2,10},{4,12},{5,13},{7,15},{6,14},{16,24},{17,... | collective-permute-start | bytes 5111816 | tf_op jit(solution)/shard_map/ppermute | solution.py:111
  59.5 3.6 %collective-permute-done.1.refs_1_ = bf16[512,1664]{1,0:T(8,128)(2,1)S(1)} collective-permute-done((bf16[512,1664]{1,0:T(8,128)(2,1)S(1)}, bf16[512,1664]{1,0:T(8,128)(2,1)S(1)}, u32[]{:S(2)}, u32[]{:S(2)}) %collective-permute-start.1) | collective-permute-done | bytes 1703968 | tf_op jit(solution)/shard_map/ppermute | solution.py:111
  63.1 2.1 %shard_map.104 = f32[512,768]{1,0:T(8,128)S(1)} custom-call(bf16[512,1664]{1,0:T(8,128)(2,1)S(1)} %bitcast.27, bf16[512,1664]{1,0:T(8,128)(2,1)S(1)} %collective-permute-done.1.refs_1_), custom_call_target="tpu_custom_call" | custom-call | tf_op jit(solution)/shard_map/pallas_call | solution.py:50
  65.2 1.0 %convert_element_type.53 = f16[512,768]{1,0:T(8,128)(2,1)} convert(f32[512,768]{1,0:T(8,128)S(1)} %shard_map.104) | non-fusion elementwise | flops 393216 | bytes 2359296 | tf_op jit(solution)/shard_map/convert_element_type | solution.py:113
  66.1 6.9 %all-to-all-start.2 = ((f16[16,32,768]{2,1,0:T(8,128)(2,1)}), f16[16,32,768]{2,1,0:T(8,128)(2,1)S(1)}, u32[]{:S(2)}, u32[]{:S(2)}) async-start(f16[16,32,768]{2,1,0:T(8,128)(2,1)} %bitcast.7), calls=%async_computation.2 | async-start | bytes 1572864 | tf_op jit(solution)/shard_map/all_to_all | solution.py:114
  73.0 15.8 %all-to-all-done.2 = f16[16,32,768]{2,1,0:T(8,128)(2,1)S(1)} async-done(((f16[16,32,768]{2,1,0:T(8,128)(2,1)}), f16[16,32,768]{2,1,0:T(8,128)(2,1)S(1)}, u32[]{:S(2)}, u32[]{:S(2)}) %all-to-all-start.2) | async-done | bytes 786464 | tf_op jit(solution)/shard_map/all_to_all | solution.py:114
  88.9 0.1 convert_reduce_fusion
  89.0 1.9 %all-gather = f32[64,768]{1,0:T(8,128)S(1)} all-gather(f32[32,768]{1,0:T(8,128)S(1)} %broadcast_multiply_fusion), channel_id=2, replica_groups={{0,8},{1,9},{3,11},{2,10},{4,12},{5,13},{7,15},{6,14},{16,24},{17,25},{..., dimensions={0}, use_global_device_ids=true | all-gather | bytes 294912 | tf_op jit(solution)/shard_map/all_gather | solution.py:116
  91.0 0.6 dynamic-slice_bitcast_fusion
  (9 shorter events, 0.1 us)
Async XLA Ops:
  0.6 1.0 %copy-start = (bf16[256,768]{1,0:T(8,128)(2,1)S(1)}, bf16[256,768]{1,0:T(8,128)(2,1)}, u32[]{:S(2)}) copy-start(bf16[256,768]{1,0:T(8,128)(2,1)} %param.11) | copy-start | bytes 1179652
  2.7 12.5 %copy-start.4 = (s32[128]{0:T(128)S(1)}, s32[128]{0:T(128)}, u32[]{:S(2)}) copy-start(s32[128]{0:T(128)} %param.17) | copy-start | bytes 1540
  2.7 13.6 %copy-start.1 = (bf16[16,768]{1,0:T(8,128)(2,1)S(1)}, bf16[16,768]{1,0:T(8,128)(2,1)}, u32[]{:S(2)}) copy-start(bf16[16,768]{1,0:T(8,128)(2,1)} %param.14) | copy-start | bytes 73732
  4.0 14.5 %copy-start.2 = (s32[768]{0:T(1024)S(1)}, s32[768]{0:T(1024)}, u32[]{:S(2)}) copy-start(s32[768]{0:T(1024)} %param.15) | copy-start | bytes 9220
  4.0 14.5 %copy-start.3 = (s32[768]{0:T(1024)S(1)}, s32[768]{0:T(1024)}, u32[]{:S(2)}) copy-start(s32[768]{0:T(1024)} %param.16) | copy-start | bytes 9220
  4.9 19.4 %all-to-all-start = ((f16[16,16,768]{2,1,0:T(8,128)(2,1)}), f16[16,16,768]{2,1,0:T(8,128)(2,1)S(1)}, u32[]{:S(2)}, u32[]{:S(2)}) async-start(f16[16,16,768]{2,1,0:T(8,128)(2,1)} %pad_maximum_fusion), calls=%async_computation | async-start | bytes 786432 | tf_op jit(solution)/shard_map/all_to_all | solution.py:102
  16.4 3.1 %collective-permute-start = (bf16[16,896]{1,0:T(8,128)(2,1)S(1)}, bf16[16,896]{1,0:T(8,128)(2,1)S(1)}, u32[]{:S(2)}, u32[]{:S(2)}) collective-permute-start(bf16[16,896]{1,0:T(8,128)(2,1)S(1)} %broadcast_select_fusion.2), channel_id=1, source_target_pairs={{0,8},{1,9},{3,11},{2,10},{4,12},{5,13},{7,15},{6,14},{16,24},{17,... | collective-permute-start | bytes 86024 | tf_op jit(solution)/shard_map/ppermute | solution.py:94
  57.6 5.5 %collective-permute-start.1 = (bf16[512,1664]{1,0:T(8,128)(2,1)S(1)}, bf16[512,1664]{1,0:T(8,128)(2,1)S(1)}, u32[]{:S(2)}, u32[]{:S(2)}) collective-permute-start(bf16[512,1664]{1,0:T(8,128)(2,1)S(1)} %bitcast.26), channel_id=1, source_target_pairs={{0,8},{1,9},{3,11},{2,10},{4,12},{5,13},{7,15},{6,14},{16,24},{17,... | collective-permute-start | bytes 5111816 | tf_op jit(solution)/shard_map/ppermute | solution.py:111
  66.1 22.8 %all-to-all-start.2 = ((f16[16,32,768]{2,1,0:T(8,128)(2,1)}), f16[16,32,768]{2,1,0:T(8,128)(2,1)S(1)}, u32[]{:S(2)}, u32[]{:S(2)}) async-start(f16[16,32,768]{2,1,0:T(8,128)(2,1)} %bitcast.7), calls=%async_computation.2 | async-start | bytes 1572864 | tf_op jit(solution)/shard_map/all_to_all | solution.py:114

commit v3 on v2

--- a/solution.py
+++ b/solution.py
@@ -15,44 +15,35 @@
 AXES = ("dp", "mp")
 
 
-def pair_kernel(factor, width, mine, other, out, held, sems):
-    ahead = [
-        pltpu.make_async_copy(other.at[:, cols], held.at[:, cols], sems.at[i])
-        for i, cols in enumerate((pl.ds(width, width + 128), pl.ds(0, width)))
-    ]
-    for copy in ahead:
-        copy.start()
+def pair_kernel(factor, width, mine, other, out):
     inner = (((1,), (1,)), ((), ()))
     size = mine.shape[0] // 2
     lane = lax.broadcasted_iota(jnp.int32, (8, 128), 1)
     weigh = jnp.where(lane == 0, 128.0, jnp.where(lane == 1, 1.0, 0.0)).astype(jnp.bfloat16)
-    ahead[0].wait()
-    tag_other = lax.dot_general(weigh, held[:, 2 * width :], inner, preferred_element_type=jnp.float32)[0:1]
+    tag_other = lax.dot_general(weigh, other[:, 2 * width :], inner, preferred_element_type=jnp.float32)[0:1]
     targets = []
     for start in (0, size):
         at = pl.ds(start, size)
         teacher = lax.dot_general(
-            mine[at, width : 2 * width], held[:, width : 2 * width], inner, preferred_element_type=jnp.float32
+            mine[at, width : 2 * width], other[:, width : 2 * width], inner, preferred_element_type=jnp.float32
         )
         tags = mine[at, 2 * width :].astype(jnp.float32)
         tag_mine = 128.0 * tags[:, 0:1] + tags[:, 1:2]
         hard = jnp.where(tag_mine == tag_other, 0.5, 0.0)
         targets.append(0.25 * jnp.tanh((0.5 * factor) * teacher) - 0.25 + hard)
-    ahead[1].wait()
     for start, target in zip((0, size), targets):
         at = pl.ds(start, size)
-        student = lax.dot_general(mine[at, :width], held[:, :width], inner, preferred_element_type=jnp.float32)
+        student = lax.dot_general(mine[at, :width], other[:, :width], inner, preferred_element_type=jnp.float32)
         grads = 0.5 * jnp.tanh((0.5 * factor) * student + 0.5 * LOGIT_SHIFT) - target
-        out[at, :] = jnp.dot(grads.astype(jnp.bfloat16), held[:, :width], preferred_element_type=jnp.float32)
+        out[at, :] = jnp.dot(grads.astype(jnp.bfloat16), other[:, :width], preferred_element_type=jnp.float32)
 
 
 def pair_grads(mine, other, factor, width):
     return pl.pallas_call(
         lambda *refs: pair_kernel(factor, width, *refs),
         out_shape=jax.ShapeDtypeStruct((mine.shape[0], width), jnp.float32),
-        in_specs=[pl.BlockSpec(memory_space=pltpu.VMEM), pl.BlockSpec(memory_space=pl.ANY)],
+        in_specs=[pl.BlockSpec(memory_space=pltpu.VMEM)] * 2,
         out_specs=pl.BlockSpec(memory_space=pltpu.VMEM),
-        scratch_shapes=[pltpu.VMEM(other.shape, other.dtype), pltpu.SemaphoreType.DMA((2,))],
         compiler_params=pltpu.CompilerParams(vmem_limit_bytes=32 * 2**20),
     )(mine, other)
 
@@ -114,8 +105,7 @@
     acc = lax.all_to_all(acc.reshape(16, 2 * rows, width), AXES, 0, 0, axis_index_groups=grid)
     acc = factor * acc.astype(jnp.float32).sum(0)
     both = lax.all_gather(acc, AXES, axis=0, axis_index_groups=pairs).reshape(2, 2, rows, width)
-    own = lax.dynamic_index_in_dim(both, dp_index % 2, 1, keepdims=False)
-    return own[0], own[1]
+    return tuple(jnp.where(even, side[0], side[1]) for side in both)
 
 
 def solution(mesh):

time: 92.2 us -> 91.2 us (0.989)
  blocking collectives: 35 us -> 58.1 us
  waiting for transfers between devices: 25.1 us -> 9.27 us
  starting transfers between devices: 21.2 us -> 14.3 us
    all_to_all x0 -> x1, blocking collectives: none -> 23.1 us  [body(): lax.all_to_all(acc.reshape(16, 2 * rows, width), AXES, 0, 0, axis_index_g...]
    all_to_all x1 -> x0, waiting for transfers between devices: 15.8 us -> none  [body(): lax.all_to_all(acc.reshape(16, 2 * rows, width), AXES, 0, 0, axis_index_g...]
    all_to_all x1 -> x0, starting transfers between devices: 6.9 us -> none  [body(): lax.all_to_all(acc.reshape(16, 2 * rows, width), AXES, 0, 0, axis_index_g...]
  transfers between devices with their start and end apart: 4 -> 3, of which waited for: 4 -> 3; matrix products, arithmetic and copies ran while one was open for 1% -> 1% of each run, Pallas kernels for 0% -> 0%
where the time goes in v3:
time: 91.2 us; the launch traced here: 90.7 us
  blocking collectives  58.1 us (64%)
  starting transfers between devices  14.3 us (16%)
  waiting for transfers between devices  9.27 us (10%)
  matrix products  2.3 us (3%)
  local copies, waits for them, and re-layouts  2.16 us (2%)
  other arithmetic  2.11 us (2%)
  Pallas kernels  1.7 us (2%)
    all_to_all x1, blocking collectives, body(): lax.all_to_all(jnp.broadcast_to(mine[None], (16,) + mine.shape), AXES, 0,...  33 us
    all_to_all x1, blocking collectives, body(): lax.all_to_all(acc.reshape(16, 2 * rows, width), AXES, 0, 0, axis_index_g...  23.1 us
    all_to_all x1, starting transfers between devices, body(): parts = lax.all_to_all(parts, AXES, 0, 0, axis_index_groups=core_mp)  10.3 us
    all_to_all x1, waiting for transfers between devices, body(): parts = lax.all_to_all(parts, AXES, 0, 0, axis_index_groups=core_mp)  4.76 us
    ppermute x1, waiting for transfers between devices, body(): other = lax.ppermute(mine, AXES, swap)  3.56 us
    ppermute x1, starting transfers between devices, body(): got = lax.ppermute(jnp.where(even, t_pep, t_spec), AXES, swap)  2.09 us
    all_gather x1, blocking collectives, body(): lax.all_gather(acc, AXES, axis=0, axis_index_groups=pairs)  1.95 us
    ppermute x1, starting transfers between devices, body(): other = lax.ppermute(mine, AXES, swap)  1.91 us
  transfers between devices with their start and end apart: 3, of which 3 were waited for; matrix products, arithmetic and copies ran while one was open for 1% of the time, Pallas kernels for 0%

profile of v3, /device:TPU:1, one launch (start us, length us, event | category | flops | bytes accessed | tf_op | source)
XLA Modules:
  0.0 90.7 jit_solution(93309988816369529)
XLA Ops:
  0.6 0.0 copy-start
  0.6 1.0 %copy-done = bf16[256,768]{1,0:T(8,128)(2,1)S(1)} copy-done((bf16[256,768]{1,0:T(8,128)(2,1)S(1)}, bf16[256,768]{1,0:T(8,128)(2,1)}, u32[]{:S(2)}) %copy-start) | copy-done | bytes 393240
  1.6 1.0 %fusion.14 = f32[128,768]{1,0:T(8,128)S(1)} fusion(bf16[128,256]{1,0:T(8,128)(2,1)} %param.9, bf16[256,768]{1,0:T(8,128)(2,1)S(1)} %copy-done), kind=kOutput, calls=%fused_computation.43 | convolution fusion | flops 50331648 | bytes 851968 | tf_op jit(solution)/shard_map/dot_general | solution.py:88
  2.7 0.0 copy-start.4
  2.7 0.0 copy-start.1
  2.7 1.3 %fusion.15 = f32[128,768]{1,0:T(8,128)S(1)} fusion(bf16[128,256]{1,0:T(8,128)(2,1)} %param.10, bf16[256,768]{1,0:T(8,128)(2,1)} %param.12), kind=kOutput, calls=%fused_computation.44 | convolution fusion | flops 50331648 | bytes 851968 | tf_op jit(solution)/shard_map/dot_general | solution.py:89
  4.0 0.0 copy-start.2
  4.0 0.0 copy-start.3
  4.1 0.8 pad_maximum_fusion
  4.9 10.3 %all-to-all-start = ((f16[16,16,768]{2,1,0:T(8,128)(2,1)}), f16[16,16,768]{2,1,0:T(8,128)(2,1)S(1)}, u32[]{:S(2)}, u32[]{:S(2)}) async-start(f16[16,16,768]{2,1,0:T(8,128)(2,1)} %pad_maximum_fusion), calls=%async_computation | async-start | bytes 786432 | tf_op jit(solution)/shard_map/all_to_all | solution.py:93
  15.2 0.0 copy-done.4
  15.2 0.1 convert_bitcast_fusion
  15.3 0.1 copy.12
  15.4 0.1 copy.11
  15.5 0.7 constant_dynamic-slice_fusion
  16.2 0.1 pad.10.clone
  16.3 0.0 copy-done.1
  16.3 0.1 broadcast_select_fusion.2
  16.4 2.1 %collective-permute-start = (bf16[16,896]{1,0:T(8,128)(2,1)S(1)}, bf16[16,896]{1,0:T(8,128)(2,1)S(1)}, u32[]{:S(2)}, u32[]{:S(2)}) collective-permute-start(bf16[16,896]{1,0:T(8,128)(2,1)S(1)} %broadcast_select_fusion.2), channel_id=1, source_target_pairs={{0,8},{1,9},{3,11},{2,10},{4,12},{5,13},{7,15},{6,14},{16,24},{17,... | collective-permute-start | bytes 86024 | tf_op jit(solution)/shard_map/ppermute | solution.py:85
  18.5 0.0 copy-done.2
  18.5 0.0 copy-done.3
  18.5 0.9 %collective-permute-done = bf16[16,896]{1,0:T(8,128)(2,1)S(1)} collective-permute-done((bf16[16,896]{1,0:T(8,128)(2,1)S(1)}, bf16[16,896]{1,0:T(8,128)(2,1)S(1)}, u32[]{:S(2)}, u32[]{:S(2)}) %collective-permute-start) | collective-permute-done | bytes 28704 | tf_op jit(solution)/shard_map/ppermute | solution.py:85
  19.5 0.1 broadcast_select_fusion.1
  19.6 4.8 %all-to-all-done = f16[16,16,768]{2,1,0:T(8,128)(2,1)S(1)} async-done(((f16[16,16,768]{2,1,0:T(8,128)(2,1)}), f16[16,16,768]{2,1,0:T(8,128)(2,1)S(1)}, u32[]{:S(2)}, u32[]{:S(2)}) %all-to-all-start) | async-done | bytes 393248 | tf_op jit(solution)/shard_map/all_to_all | solution.py:93
  24.3 0.1 convert_reduce_fusion.1
  24.4 0.1 broadcast_in_dim.20
  24.5 33.0 %all_to_all.15 = bf16[16,32,1664]{2,1,0:T(8,128)(2,1)S(1)} all-to-all(bf16[16,32,1664]{2,1,0:T(8,128)(2,1)S(1)} %broadcast_in_dim.20), channel_id=1, replica_groups={{0,1,4,5,128,129,132,133,256,257,260,261,384,385,388,389},{3,2,7,6,131,..., dimensions={0} | all-to-all | bytes 3407872 | tf_op jit(solution)/shard_map/all_to_all | solution.py:99
  57.6 1.9 %collective-permute-start.1 = (bf16[512,1664]{1,0:T(8,128)(2,1)S(1)}, bf16[512,1664]{1,0:T(8,128)(2,1)S(1)}, u32[]{:S(2)}, u32[]{:S(2)}) collective-permute-start(bf16[512,1664]{1,0:T(8,128)(2,1)S(1)} %bitcast.26), channel_id=1, source_target_pairs={{0,8},{1,9},{3,11},{2,10},{4,12},{5,13},{7,15},{6,14},{16,24},{17,... | collective-permute-start | bytes 5111816 | tf_op jit(solution)/shard_map/ppermute | solution.py:102
  59.5 3.6 %collective-permute-done.1.refs_1_ = bf16[512,1664]{1,0:T(8,128)(2,1)S(1)} collective-permute-done((bf16[512,1664]{1,0:T(8,128)(2,1)S(1)}, bf16[512,1664]{1,0:T(8,128)(2,1)S(1)}, u32[]{:S(2)}, u32[]{:S(2)}) %collective-permute-start.1) | collective-permute-done | bytes 1703968 | tf_op jit(solution)/shard_map/ppermute | solution.py:102
  63.1 1.7 %shard_map.104 = f32[512,768]{1,0:T(8,128)S(1)} custom-call(bf16[512,1664]{1,0:T(8,128)(2,1)S(1)} %bitcast.27, bf16[512,1664]{1,0:T(8,128)(2,1)S(1)} %collective-permute-done.1.refs_1_), custom_call_target="tpu_custom_call" | custom-call | tf_op jit(solution)/shard_map/pallas_call | solution.py:42
  64.8 0.1 convert_element_type.53
  64.9 23.1 %all_to_all.16 = f16[16,32,768]{2,1,0:T(8,128)(2,1)S(1)} all-to-all(f16[16,32,768]{2,1,0:T(8,128)(2,1)S(1)} %bitcast.28), channel_id=1, replica_groups={{0,1,4,5,128,129,132,133,256,257,260,261,384,385,388,389},{3,2,7,6,131,..., dimensions={0} | all-to-all | bytes 1572864 | tf_op jit(solution)/shard_map/all_to_all | solution.py:105
  88.0 0.1 convert_reduce_fusion
  88.1 1.9 %all-gather = f32[64,768]{1,0:T(8,128)S(1)} all-gather(f32[32,768]{1,0:T(8,128)S(1)} %broadcast_multiply_fusion), channel_id=2, replica_groups={{0,8},{1,9},{3,11},{2,10},{4,12},{5,13},{7,15},{6,14},{16,24},{17,25},{..., dimensions={0}, use_global_device_ids=true | all-gather | bytes 294912 | tf_op jit(solution)/shard_map/all_gather | solution.py:107
  90.1 0.6 fusion.2
  (9 shorter events, 0.1 us)
Async XLA Ops:
  0.6 1.0 %copy-start = (bf16[256,768]{1,0:T(8,128)(2,1)S(1)}, bf16[256,768]{1,0:T(8,128)(2,1)}, u32[]{:S(2)}) copy-start(bf16[256,768]{1,0:T(8,128)(2,1)} %param.11) | copy-start | bytes 1179652
  2.7 12.5 %copy-start.4 = (s32[128]{0:T(128)S(1)}, s32[128]{0:T(128)}, u32[]{:S(2)}) copy-start(s32[128]{0:T(128)} %param.17) | copy-start | bytes 1540
  2.7 13.6 %copy-start.1 = (bf16[16,768]{1,0:T(8,128)(2,1)S(1)}, bf16[16,768]{1,0:T(8,128)(2,1)}, u32[]{:S(2)}) copy-start(bf16[16,768]{1,0:T(8,128)(2,1)} %param.14) | copy-start | bytes 73732
  4.0 14.5 %copy-start.2 = (s32[768]{0:T(1024)S(1)}, s32[768]{0:T(1024)}, u32[]{:S(2)}) copy-start(s32[768]{0:T(1024)} %param.15) | copy-start | bytes 9220
  4.0 14.5 %copy-start.3 = (s32[768]{0:T(1024)S(1)}, s32[768]{0:T(1024)}, u32[]{:S(2)}) copy-start(s32[768]{0:T(1024)} %param.16) | copy-start | bytes 9220
  4.9 19.4 %all-to-all-start = ((f16[16,16,768]{2,1,0:T(8,128)(2,1)}), f16[16,16,768]{2,1,0:T(8,128)(2,1)S(1)}, u32[]{:S(2)}, u32[]{:S(2)}) async-start(f16[16,16,768]{2,1,0:T(8,128)(2,1)} %pad_maximum_fusion), calls=%async_computation | async-start | bytes 786432 | tf_op jit(solution)/shard_map/all_to_all | solution.py:93
  16.4 3.1 %collective-permute-start = (bf16[16,896]{1,0:T(8,128)(2,1)S(1)}, bf16[16,896]{1,0:T(8,128)(2,1)S(1)}, u32[]{:S(2)}, u32[]{:S(2)}) collective-permute-start(bf16[16,896]{1,0:T(8,128)(2,1)S(1)} %broadcast_select_fusion.2), channel_id=1, source_target_pairs={{0,8},{1,9},{3,11},{2,10},{4,12},{5,13},{7,15},{6,14},{16,24},{17,... | collective-permute-start | bytes 86024 | tf_op jit(solution)/shard_map/ppermute | solution.py:85
  57.6 5.5 %collective-permute-start.1 = (bf16[512,1664]{1,0:T(8,128)(2,1)S(1)}, bf16[512,1664]{1,0:T(8,128)(2,1)S(1)}, u32[]{:S(2)}, u32[]{:S(2)}) collective-permute-start(bf16[512,1664]{1,0:T(8,128)(2,1)S(1)} %bitcast.26), channel_id=1, source_target_pairs={{0,8},{1,9},{3,11},{2,10},{4,12},{5,13},{7,15},{6,14},{16,24},{17,... | collective-permute-start | bytes 5111816 | tf_op jit(solution)/shard_map/ppermute | solution.py:102

commit v4 on v3

--- a/solution.py
+++ b/solution.py
@@ -85,11 +85,13 @@
     got = lax.ppermute(jnp.where(even, t_pep, t_spec), AXES, swap)
     teach_rows = jnp.concatenate([jnp.where(even, keep, got), jnp.where(even, got, keep)], 0)
 
-    part_spec = jnp.dot(spec_feat, w_spec, preferred_element_type=jnp.float32)
-    part_pep = jnp.dot(pep_feat, w_pep, preferred_element_type=jnp.float32)
-    part_spec, part_pep = lax.optimization_barrier((part_spec, part_pep))
-    parts = jnp.concatenate([part_spec.reshape(8, rows, width), part_pep.reshape(8, rows, width)], 0)
-    parts = parts.astype(jnp.float16)
+    parts = lax.dot_general(
+        jnp.stack([spec_feat, pep_feat]),
+        jnp.stack([w_spec, w_pep]),
+        (((2,), (1,)), ((0,), (0,))),
+        preferred_element_type=jnp.float32,
+    )
+    parts = parts.astype(jnp.float16).reshape(16, rows, width)
     parts = lax.all_to_all(parts, AXES, 0, 0, axis_index_groups=core_mp)
     sums = parts.reshape(2, 8, rows, width).astype(jnp.float32).sum(1).reshape(2 * rows, width)
     limits = CLIP_LEVELS * jnp.exp2(-jnp.where(even, exp_spec, exp_pep).astype(jnp.float32))

time: 91.2 us -> 89.2 us (0.978)
  local copies, waits for them, and re-layouts: 2.16 us -> 0.42 us
    unnamed x10, local copies, waits for them, and re-layouts: 1.02 us -> 0.03 us
    dot_general x2 -> x1, matrix products: 2.3 us -> 2.31 us  [body(): lax.dot_general(jnp.stack([spec_feat, pep_feat]), jnp.stack([w_spec, w_pe...]
where the time goes in v4:
time: 89.2 us; the launch traced here: 88.8 us
  blocking collectives  58.1 us (65%)
  starting transfers between devices  14.3 us (16%)
  waiting for transfers between devices  10 us (11%)
  matrix products  2.31 us (3%)
  Pallas kernels  1.71 us (2%)
  other arithmetic  1.23 us (1%)
    all_to_all x1, blocking collectives, body(): lax.all_to_all(jnp.broadcast_to(mine[None], (16,) + mine.shape), AXES, 0,...  33 us
    all_to_all x1, blocking collectives, body(): lax.all_to_all(acc.reshape(16, 2 * rows, width), AXES, 0, 0, axis_index_g...  23.1 us
    all_to_all x1, starting transfers between devices, body(): parts = lax.all_to_all(parts, AXES, 0, 0, axis_index_groups=core_mp)  10.3 us
    all_to_all x1, waiting for transfers between devices, body(): parts = lax.all_to_all(parts, AXES, 0, 0, axis_index_groups=core_mp)  5.49 us
    ppermute x1, waiting for transfers between devices, body(): other = lax.ppermute(mine, AXES, swap)  3.56 us
    dot_general x1, matrix products, body(): lax.dot_general(jnp.stack([spec_feat, pep_feat]), jnp.stack([w_spec, w_pe...  2.31 us
    ppermute x1, starting transfers between devices, body(): got = lax.ppermute(jnp.where(even, t_pep, t_spec), AXES, swap)  2.09 us
    all_gather x1, blocking collectives, body(): lax.all_gather(acc, AXES, axis=0, axis_index_groups=pairs)  1.95 us
  transfers between devices with their start and end apart: 3, of which 3 were waited for; matrix products, arithmetic and copies ran while one was open for 1% of the time, Pallas kernels for 0%

profile of v4, /device:TPU:1, one launch (start us, length us, event | category | flops | bytes accessed | tf_op | source)
XLA Modules:
  0.0 88.8 jit_solution(4564196691454413597)
XLA Ops:
  0.6 0.0 copy-start
  0.6 0.0 copy-start.4
  0.7 0.0 copy-start.1
  0.7 0.0 copy-start.3
  0.7 0.0 copy-start.2
  0.7 2.3 %convolution_convert_fusion = f16[2,128,768]{2,1,0:T(8,128)(2,1)} fusion(bf16[1,256,768]{2,1,0:T(8,128)(2,1)} %bitcast.29, bf16[1,256,768]{2,1,0:T(8,128)(2,1)} %bitcast.30, bf16[1,128,256]{2,1,0:T(8,128)(2,1)} %bitcast.31, bf16[1,128,256]{2,1,0:T(8,128)(2,1)} %bitcast.32), kind=kOutput, calls=%fused_computation.1 | convolution fusion | flops 101318656 | bytes 1310720 | tf_op jit(solution)/shard_map/dot_general | solution.py:88
  3.0 10.3 %all-to-all-start = ((f16[16,16,768]{2,1,0:T(8,128)(2,1)}), f16[16,16,768]{2,1,0:T(8,128)(2,1)S(1)}, u32[]{:S(2)}, u32[]{:S(2)}) async-start(f16[16,16,768]{2,1,0:T(8,128)(2,1)} %bitcast.4), calls=%async_computation | async-start | bytes 786432 | tf_op jit(solution)/shard_map/all_to_all | solution.py:95
  13.3 0.0 copy-done.4
  13.3 0.1 convert_bitcast_fusion
  13.4 0.1 copy.12
  13.5 0.1 copy.11
  13.6 0.0 copy-done
  13.6 0.1 pad.10.clone
  13.7 0.0 copy-done.1
  13.7 0.1 broadcast_select_fusion.2
  13.8 2.1 %collective-permute-start = (bf16[16,896]{1,0:T(8,128)(2,1)S(1)}, bf16[16,896]{1,0:T(8,128)(2,1)S(1)}, u32[]{:S(2)}, u32[]{:S(2)}) collective-permute-start(bf16[16,896]{1,0:T(8,128)(2,1)S(1)} %broadcast_select_fusion.2), channel_id=1, source_target_pairs={{0,8},{1,9},{3,11},{2,10},{4,12},{5,13},{7,15},{6,14},{16,24},{17,... | collective-permute-start | bytes 86024 | tf_op jit(solution)/shard_map/ppermute | solution.py:85
  15.9 0.0 copy-done.3
  15.9 0.0 copy-done.2
  15.9 0.9 %collective-permute-done = bf16[16,896]{1,0:T(8,128)(2,1)S(1)} collective-permute-done((bf16[16,896]{1,0:T(8,128)(2,1)S(1)}, bf16[16,896]{1,0:T(8,128)(2,1)S(1)}, u32[]{:S(2)}, u32[]{:S(2)}) %collective-permute-start) | collective-permute-done | bytes 28704 | tf_op jit(solution)/shard_map/ppermute | solution.py:85
  16.9 0.1 broadcast_select_fusion.1
  16.9 5.5 %all-to-all-done = f16[16,16,768]{2,1,0:T(8,128)(2,1)S(1)} async-done(((f16[16,16,768]{2,1,0:T(8,128)(2,1)}), f16[16,16,768]{2,1,0:T(8,128)(2,1)S(1)}, u32[]{:S(2)}, u32[]{:S(2)}) %all-to-all-start) | async-done | bytes 393248 | tf_op jit(solution)/shard_map/all_to_all | solution.py:95
  22.4 0.1 convert_reduce_fusion.1
  22.5 0.1 broadcast_in_dim.20
  22.6 33.0 %all_to_all.15 = bf16[16,32,1664]{2,1,0:T(8,128)(2,1)S(1)} all-to-all(bf16[16,32,1664]{2,1,0:T(8,128)(2,1)S(1)} %broadcast_in_dim.20), channel_id=1, replica_groups={{0,1,4,5,128,129,132,133,256,257,260,261,384,385,388,389},{3,2,7,6,131,..., dimensions={0} | all-to-all | bytes 3407872 | tf_op jit(solution)/shard_map/all_to_all | solution.py:101
  55.7 1.9 %collective-permute-start.1 = (bf16[512,1664]{1,0:T(8,128)(2,1)S(1)}, bf16[512,1664]{1,0:T(8,128)(2,1)S(1)}, u32[]{:S(2)}, u32[]{:S(2)}) collective-permute-start(bf16[512,1664]{1,0:T(8,128)(2,1)S(1)} %bitcast.25), channel_id=1, source_target_pairs={{0,8},{1,9},{3,11},{2,10},{4,12},{5,13},{7,15},{6,14},{16,24},{17,... | collective-permute-start | bytes 5111816 | tf_op jit(solution)/shard_map/ppermute | solution.py:104
  57.6 3.6 %collective-permute-done.1.refs_1_ = bf16[512,1664]{1,0:T(8,128)(2,1)S(1)} collective-permute-done((bf16[512,1664]{1,0:T(8,128)(2,1)S(1)}, bf16[512,1664]{1,0:T(8,128)(2,1)S(1)}, u32[]{:S(2)}, u32[]{:S(2)}) %collective-permute-start.1) | collective-permute-done | bytes 1703968 | tf_op jit(solution)/shard_map/ppermute | solution.py:104
  61.2 1.7 %shard_map.104 = f32[512,768]{1,0:T(8,128)S(1)} custom-call(bf16[512,1664]{1,0:T(8,128)(2,1)S(1)} %bitcast.26, bf16[512,1664]{1,0:T(8,128)(2,1)S(1)} %collective-permute-done.1.refs_1_), custom_call_target="tpu_custom_call" | custom-call | tf_op jit(solution)/shard_map/pallas_call | solution.py:42
  62.9 0.1 convert_element_type.56
  63.0 23.1 %all_to_all.16 = f16[16,32,768]{2,1,0:T(8,128)(2,1)S(1)} all-to-all(f16[16,32,768]{2,1,0:T(8,128)(2,1)S(1)} %bitcast.27), channel_id=1, replica_groups={{0,1,4,5,128,129,132,133,256,257,260,261,384,385,388,389},{3,2,7,6,131,..., dimensions={0} | all-to-all | bytes 1572864 | tf_op jit(solution)/shard_map/all_to_all | solution.py:107
  86.1 0.1 convert_reduce_fusion
  86.2 1.9 %all-gather = f32[64,768]{1,0:T(8,128)S(1)} all-gather(f32[32,768]{1,0:T(8,128)S(1)} %broadcast_multiply_fusion), channel_id=2, replica_groups={{0,8},{1,9},{3,11},{2,10},{4,12},{5,13},{7,15},{6,14},{16,24},{17,25},{..., dimensions={0}, use_global_device_ids=true | all-gather | bytes 294912 | tf_op jit(solution)/shard_map/all_gather | solution.py:109
  88.2 0.6 fusion.8
  (8 shorter events, 0.1 us)
Async XLA Ops:
  0.6 12.9 %copy-start = (bf16[128,768]{1,0:T(8,128)(2,1)S(1)}, bf16[128,768]{1,0:T(8,128)(2,1)}, u32[]{:S(2)}) copy-start(bf16[128,768]{1,0:T(8,128)(2,1)} %param.13) | copy-start | bytes 589828
  0.6 12.6 %copy-start.4 = (s32[128]{0:T(128)S(1)}, s32[128]{0:T(128)}, u32[]{:S(2)}) copy-start(s32[128]{0:T(128)} %param.17) | copy-start | bytes 1540
  0.7 13.0 %copy-start.1 = (bf16[16,768]{1,0:T(8,128)(2,1)S(1)}, bf16[16,768]{1,0:T(8,128)(2,1)}, u32[]{:S(2)}) copy-start(bf16[16,768]{1,0:T(8,128)(2,1)} %param.14) | copy-start | bytes 73732
  0.7 15.2 %copy-start.3 = (s32[768]{0:T(1024)S(1)}, s32[768]{0:T(1024)}, u32[]{:S(2)}) copy-start(s32[768]{0:T(1024)} %param.16) | copy-start | bytes 9220
  0.7 15.2 %copy-start.2 = (s32[768]{0:T(1024)S(1)}, s32[768]{0:T(1024)}, u32[]{:S(2)}) copy-start(s32[768]{0:T(1024)} %param.15) | copy-start | bytes 9220
  3.0 19.4 %all-to-all-start = ((f16[16,16,768]{2,1,0:T(8,128)(2,1)}), f16[16,16,768]{2,1,0:T(8,128)(2,1)S(1)}, u32[]{:S(2)}, u32[]{:S(2)}) async-start(f16[16,16,768]{2,1,0:T(8,128)(2,1)} %bitcast.4), calls=%async_computation | async-start | bytes 786432 | tf_op jit(solution)/shard_map/all_to_all | solution.py:95
  13.8 3.1 %collective-permute-start = (bf16[16,896]{1,0:T(8,128)(2,1)S(1)}, bf16[16,896]{1,0:T(8,128)(2,1)S(1)}, u32[]{:S(2)}, u32[]{:S(2)}) collective-permute-start(bf16[16,896]{1,0:T(8,128)(2,1)S(1)} %broadcast_select_fusion.2), channel_id=1, source_target_pairs={{0,8},{1,9},{3,11},{2,10},{4,12},{5,13},{7,15},{6,14},{16,24},{17,... | collective-permute-start | bytes 86024 | tf_op jit(solution)/shard_map/ppermute | solution.py:85
  55.7 5.5 %collective-permute-start.1 = (bf16[512,1664]{1,0:T(8,128)(2,1)S(1)}, bf16[512,1664]{1,0:T(8,128)(2,1)S(1)}, u32[]{:S(2)}, u32[]{:S(2)}) collective-permute-start(bf16[512,1664]{1,0:T(8,128)(2,1)S(1)} %bitcast.25), channel_id=1, source_target_pairs={{0,8},{1,9},{3,11},{2,10},{4,12},{5,13},{7,15},{6,14},{16,24},{17,... | collective-permute-start | bytes 5111816 | tf_op jit(solution)/shard_map/ppermute | solution.py:104

commit v5 on v4

--- a/solution.py
+++ b/solution.py
@@ -54,8 +54,8 @@
     flat = flat[..., [0, 1, 3, 2]].reshape(4, 8, 2, 2, 2, 2)
     even = flat[:, :, 0]
     odd = flat[:, :, 1]
-    spec_side = even.transpose(1, 3, 0, 2, 4).reshape(16, 16)
-    pep_side = odd.transpose(0, 2, 4, 1, 3).reshape(16, 16)
+    spec_side = even.transpose(1, 4, 3, 0, 2).reshape(16, 16)
+    pep_side = odd.transpose(0, 2, 3, 4, 1).reshape(16, 16)
     grid = np.concatenate([spec_side, pep_side], 0)
     pairs = [(int(a), int(b)) for a, b in zip(flat[:, :, 0].ravel(), flat[:, :, 1].ravel())]
     swap = pairs + [(b, a) for a, b in pairs]

time: 89.2 us -> 85.5 us (0.959)
  blocking collectives: 58.1 us -> 54.4 us
    all_to_all x1, blocking collectives: 33 us -> 30.7 us  [body(): lax.all_to_all(jnp.broadcast_to(mine[None], (16,) + mine.shape), AXES, 0,...]
    all_to_all x1, blocking collectives: 23.1 us -> 21.8 us  [body(): lax.all_to_all(acc.reshape(16, 2 * rows, width), AXES, 0, 0, axis_index_g...]
where the time goes in v5:
time: 85.5 us; the launch traced here: 85.1 us
  blocking collectives  54.4 us (64%)
  starting transfers between devices  14.3 us (17%)
  waiting for transfers between devices  10 us (12%)
  matrix products  2.31 us (3%)
  Pallas kernels  1.71 us (2%)
  other arithmetic  1.23 us (1%)
    all_to_all x1, blocking collectives, body(): lax.all_to_all(jnp.broadcast_to(mine[None], (16,) + mine.shape), AXES, 0,...  30.7 us
    all_to_all x1, blocking collectives, body(): lax.all_to_all(acc.reshape(16, 2 * rows, width), AXES, 0, 0, axis_index_g...  21.8 us
    all_to_all x1, starting transfers between devices, body(): parts = lax.all_to_all(parts, AXES, 0, 0, axis_index_groups=core_mp)  10.3 us
    all_to_all x1, waiting for transfers between devices, body(): parts = lax.all_to_all(parts, AXES, 0, 0, axis_index_groups=core_mp)  5.49 us
    ppermute x1, waiting for transfers between devices, body(): other = lax.ppermute(mine, AXES, swap)  3.56 us
    dot_general x1, matrix products, body(): lax.dot_general(jnp.stack([spec_feat, pep_feat]), jnp.stack([w_spec, w_pe...  2.31 us
    ppermute x1, starting transfers between devices, body(): got = lax.ppermute(jnp.where(even, t_pep, t_spec), AXES, swap)  2.09 us
    all_gather x1, blocking collectives, body(): lax.all_gather(acc, AXES, axis=0, axis_index_groups=pairs)  1.95 us
  transfers between devices with their start and end apart: 3, of which 3 were waited for; matrix products, arithmetic and copies ran while one was open for 1% of the time, Pallas kernels for 0%

profile of v5, /device:TPU:1, one launch (start us, length us, event | category | flops | bytes accessed | tf_op | source)
XLA Modules:
  0.0 85.1 jit_solution(15958496213554416785)
XLA Ops:
  0.6 0.0 copy-start
  0.6 0.0 copy-start.4
  0.7 0.0 copy-start.1
  0.7 0.0 copy-start.3
  0.7 0.0 copy-start.2
  0.7 2.3 %convolution_convert_fusion = f16[2,128,768]{2,1,0:T(8,128)(2,1)} fusion(bf16[1,256,768]{2,1,0:T(8,128)(2,1)} %bitcast.29, bf16[1,256,768]{2,1,0:T(8,128)(2,1)} %bitcast.30, bf16[1,128,256]{2,1,0:T(8,128)(2,1)} %bitcast.31, bf16[1,128,256]{2,1,0:T(8,128)(2,1)} %bitcast.32), kind=kOutput, calls=%fused_computation.1 | convolution fusion | flops 101318656 | bytes 1310720 | tf_op jit(solution)/shard_map/dot_general | solution.py:88
  3.0 10.3 %all-to-all-start = ((f16[16,16,768]{2,1,0:T(8,128)(2,1)}), f16[16,16,768]{2,1,0:T(8,128)(2,1)S(1)}, u32[]{:S(2)}, u32[]{:S(2)}) async-start(f16[16,16,768]{2,1,0:T(8,128)(2,1)} %bitcast.4), calls=%async_computation | async-start | bytes 786432 | tf_op jit(solution)/shard_map/all_to_all | solution.py:95
  13.3 0.0 copy-done.4
  13.3 0.1 convert_bitcast_fusion
  13.4 0.1 copy.12
  13.5 0.1 copy.11
  13.6 0.0 copy-done
  13.6 0.1 pad.10.clone
  13.7 0.0 copy-done.1
  13.7 0.1 broadcast_select_fusion.2
  13.8 2.1 %collective-permute-start = (bf16[16,896]{1,0:T(8,128)(2,1)S(1)}, bf16[16,896]{1,0:T(8,128)(2,1)S(1)}, u32[]{:S(2)}, u32[]{:S(2)}) collective-permute-start(bf16[16,896]{1,0:T(8,128)(2,1)S(1)} %broadcast_select_fusion.2), channel_id=1, source_target_pairs={{0,8},{1,9},{3,11},{2,10},{4,12},{5,13},{7,15},{6,14},{16,24},{17,... | collective-permute-start | bytes 86024 | tf_op jit(solution)/shard_map/ppermute | solution.py:85
  15.9 0.0 copy-done.3
  15.9 0.0 copy-done.2
  15.9 0.9 %collective-permute-done = bf16[16,896]{1,0:T(8,128)(2,1)S(1)} collective-permute-done((bf16[16,896]{1,0:T(8,128)(2,1)S(1)}, bf16[16,896]{1,0:T(8,128)(2,1)S(1)}, u32[]{:S(2)}, u32[]{:S(2)}) %collective-permute-start) | collective-permute-done | bytes 28704 | tf_op jit(solution)/shard_map/ppermute | solution.py:85
  16.9 0.1 broadcast_select_fusion.1
  16.9 5.5 %all-to-all-done = f16[16,16,768]{2,1,0:T(8,128)(2,1)S(1)} async-done(((f16[16,16,768]{2,1,0:T(8,128)(2,1)}), f16[16,16,768]{2,1,0:T(8,128)(2,1)S(1)}, u32[]{:S(2)}, u32[]{:S(2)}) %all-to-all-start) | async-done | bytes 393248 | tf_op jit(solution)/shard_map/all_to_all | solution.py:95
  22.4 0.1 convert_reduce_fusion.1
  22.5 0.1 broadcast_in_dim.20
  22.6 30.7 %all_to_all.15 = bf16[16,32,1664]{2,1,0:T(8,128)(2,1)S(1)} all-to-all(bf16[16,32,1664]{2,1,0:T(8,128)(2,1)S(1)} %broadcast_in_dim.20), channel_id=1, replica_groups={{0,4,128,132,256,260,384,388,3,7,131,135,259,263,387,391},{1,5,129,133,..., dimensions={0} | all-to-all | bytes 3407872 | tf_op jit(solution)/shard_map/all_to_all | solution.py:101
  53.3 1.9 %collective-permute-start.1 = (bf16[512,1664]{1,0:T(8,128)(2,1)S(1)}, bf16[512,1664]{1,0:T(8,128)(2,1)S(1)}, u32[]{:S(2)}, u32[]{:S(2)}) collective-permute-start(bf16[512,1664]{1,0:T(8,128)(2,1)S(1)} %bitcast.25), channel_id=1, source_target_pairs={{0,8},{1,9},{3,11},{2,10},{4,12},{5,13},{7,15},{6,14},{16,24},{17,... | collective-permute-start | bytes 5111816 | tf_op jit(solution)/shard_map/ppermute | solution.py:104
  55.2 3.6 %collective-permute-done.1.refs_1_ = bf16[512,1664]{1,0:T(8,128)(2,1)S(1)} collective-permute-done((bf16[512,1664]{1,0:T(8,128)(2,1)S(1)}, bf16[512,1664]{1,0:T(8,128)(2,1)S(1)}, u32[]{:S(2)}, u32[]{:S(2)}) %collective-permute-start.1) | collective-permute-done | bytes 1703968 | tf_op jit(solution)/shard_map/ppermute | solution.py:104
  58.8 1.7 %shard_map.104 = f32[512,768]{1,0:T(8,128)S(1)} custom-call(bf16[512,1664]{1,0:T(8,128)(2,1)S(1)} %bitcast.26, bf16[512,1664]{1,0:T(8,128)(2,1)S(1)} %collective-permute-done.1.refs_1_), custom_call_target="tpu_custom_call" | custom-call | tf_op jit(solution)/shard_map/pallas_call | solution.py:42
  60.5 0.1 convert_element_type.56
  60.6 21.8 %all_to_all.16 = f16[16,32,768]{2,1,0:T(8,128)(2,1)S(1)} all-to-all(f16[16,32,768]{2,1,0:T(8,128)(2,1)S(1)} %bitcast.27), channel_id=1, replica_groups={{0,4,128,132,256,260,384,388,3,7,131,135,259,263,387,391},{1,5,129,133,..., dimensions={0} | all-to-all | bytes 1572864 | tf_op jit(solution)/shard_map/all_to_all | solution.py:107
  82.4 0.1 convert_reduce_fusion
  82.5 1.9 %all-gather = f32[64,768]{1,0:T(8,128)S(1)} all-gather(f32[32,768]{1,0:T(8,128)S(1)} %broadcast_multiply_fusion), channel_id=2, replica_groups={{0,8},{1,9},{3,11},{2,10},{4,12},{5,13},{7,15},{6,14},{16,24},{17,25},{..., dimensions={0}, use_global_device_ids=true | all-gather | bytes 294912 | tf_op jit(solution)/shard_map/all_gather | solution.py:109
  84.5 0.6 fusion.8
  (8 shorter events, 0.1 us)
Async XLA Ops:
  0.6 12.9 %copy-start = (bf16[128,768]{1,0:T(8,128)(2,1)S(1)}, bf16[128,768]{1,0:T(8,128)(2,1)}, u32[]{:S(2)}) copy-start(bf16[128,768]{1,0:T(8,128)(2,1)} %param.13) | copy-start | bytes 589828
  0.6 12.6 %copy-start.4 = (s32[128]{0:T(128)S(1)}, s32[128]{0:T(128)}, u32[]{:S(2)}) copy-start(s32[128]{0:T(128)} %param.17) | copy-start | bytes 1540
  0.7 13.0 %copy-start.1 = (bf16[16,768]{1,0:T(8,128)(2,1)S(1)}, bf16[16,768]{1,0:T(8,128)(2,1)}, u32[]{:S(2)}) copy-start(bf16[16,768]{1,0:T(8,128)(2,1)} %param.14) | copy-start | bytes 73732
  0.7 15.2 %copy-start.3 = (s32[768]{0:T(1024)S(1)}, s32[768]{0:T(1024)}, u32[]{:S(2)}) copy-start(s32[768]{0:T(1024)} %param.16) | copy-start | bytes 9220
  0.7 15.2 %copy-start.2 = (s32[768]{0:T(1024)S(1)}, s32[768]{0:T(1024)}, u32[]{:S(2)}) copy-start(s32[768]{0:T(1024)} %param.15) | copy-start | bytes 9220
  3.0 19.4 %all-to-all-start = ((f16[16,16,768]{2,1,0:T(8,128)(2,1)}), f16[16,16,768]{2,1,0:T(8,128)(2,1)S(1)}, u32[]{:S(2)}, u32[]{:S(2)}) async-start(f16[16,16,768]{2,1,0:T(8,128)(2,1)} %bitcast.4), calls=%async_computation | async-start | bytes 786432 | tf_op jit(solution)/shard_map/all_to_all | solution.py:95
  13.8 3.1 %collective-permute-start = (bf16[16,896]{1,0:T(8,128)(2,1)S(1)}, bf16[16,896]{1,0:T(8,128)(2,1)S(1)}, u32[]{:S(2)}, u32[]{:S(2)}) collective-permute-start(bf16[16,896]{1,0:T(8,128)(2,1)S(1)} %broadcast_select_fusion.2), channel_id=1, source_target_pairs={{0,8},{1,9},{3,11},{2,10},{4,12},{5,13},{7,15},{6,14},{16,24},{17,... | collective-permute-start | bytes 86024 | tf_op jit(solution)/shard_map/ppermute | solution.py:85
  53.3 5.5 %collective-permute-start.1 = (bf16[512,1664]{1,0:T(8,128)(2,1)S(1)}, bf16[512,1664]{1,0:T(8,128)(2,1)S(1)}, u32[]{:S(2)}, u32[]{:S(2)}) collective-permute-start(bf16[512,1664]{1,0:T(8,128)(2,1)S(1)} %bitcast.25), channel_id=1, source_target_pairs={{0,8},{1,9},{3,11},{2,10},{4,12},{5,13},{7,15},{6,14},{16,24},{17,... | collective-permute-start | bytes 5111816 | tf_op jit(solution)/shard_map/ppermute | solution.py:104

commit v6 on v5

--- a/solution.py
+++ b/solution.py
@@ -12,30 +12,26 @@
 LOGIT_GAIN = 4.0
 LOGIT_SHIFT = -2.0
 CLIP_LEVELS = 127.0
+PART_SCALE = 256.0
+GRAD_SCALE = 64.0
 AXES = ("dp", "mp")
 
 
 def pair_kernel(factor, width, mine, other, out):
     inner = (((1,), (1,)), ((), ()))
-    size = mine.shape[0] // 2
     lane = lax.broadcasted_iota(jnp.int32, (8, 128), 1)
     weigh = jnp.where(lane == 0, 128.0, jnp.where(lane == 1, 1.0, 0.0)).astype(jnp.bfloat16)
     tag_other = lax.dot_general(weigh, other[:, 2 * width :], inner, preferred_element_type=jnp.float32)[0:1]
-    targets = []
-    for start in (0, size):
-        at = pl.ds(start, size)
-        teacher = lax.dot_general(
-            mine[at, width : 2 * width], other[:, width : 2 * width], inner, preferred_element_type=jnp.float32
-        )
-        tags = mine[at, 2 * width :].astype(jnp.float32)
-        tag_mine = 128.0 * tags[:, 0:1] + tags[:, 1:2]
-        hard = jnp.where(tag_mine == tag_other, 0.5, 0.0)
-        targets.append(0.25 * jnp.tanh((0.5 * factor) * teacher) - 0.25 + hard)
-    for start, target in zip((0, size), targets):
-        at = pl.ds(start, size)
-        student = lax.dot_general(mine[at, :width], other[:, :width], inner, preferred_element_type=jnp.float32)
-        grads = 0.5 * jnp.tanh((0.5 * factor) * student + 0.5 * LOGIT_SHIFT) - target
-        out[at, :] = jnp.dot(grads.astype(jnp.bfloat16), other[:, :width], preferred_element_type=jnp.float32)
+    tags = mine[:, 2 * width :].astype(jnp.float32)
+    tag_mine = 128.0 * tags[:, 0:1] + tags[:, 1:2]
+    hard = jnp.where(tag_mine == tag_other, 0.5, 0.0)
+    teacher = lax.dot_general(
+        mine[:, width : 2 * width], other[:, width : 2 * width], inner, preferred_element_type=jnp.float32
+    )
+    target = 0.25 * jnp.tanh((0.5 * factor) * teacher) - 0.25 + hard
+    student = lax.dot_general(mine[:, :width], other[:, :width], inner, preferred_element_type=jnp.float32)
+    grads = 0.5 * jnp.tanh((0.5 * factor) * student + 0.5 * LOGIT_SHIFT) - target
+    out[...] = jnp.dot(grads.astype(jnp.bfloat16), other[:, :width], preferred_element_type=jnp.float32)
 
 
 def pair_grads(mine, other, factor, width):
@@ -91,9 +87,9 @@
         (((2,), (1,)), ((0,), (0,))),
         preferred_element_type=jnp.float32,
     )
-    parts = parts.astype(jnp.float16).reshape(16, rows, width)
+    parts = (PART_SCALE * parts).astype(jnp.float16).reshape(16, rows, width)
     parts = lax.all_to_all(parts, AXES, 0, 0, axis_index_groups=core_mp)
-    sums = parts.reshape(2, 8, rows, width).astype(jnp.float32).sum(1).reshape(2 * rows, width)
+    sums = parts.reshape(2, 8, rows, width).astype(jnp.float32).sum(1).reshape(2 * rows, width) * (1.0 / PART_SCALE)
     limits = CLIP_LEVELS * jnp.exp2(-jnp.where(even, exp_spec, exp_pep).astype(jnp.float32))
     q_rows = jnp.clip(sums, -limits, limits).astype(jnp.bfloat16)
 
@@ -103,9 +99,9 @@
     ).reshape(16 * 2 * rows, -1)
     other = lax.ppermute(mine, AXES, swap)
 
-    acc = pair_grads(mine, other, factor, width).astype(jnp.float16)
+    acc = (GRAD_SCALE * pair_grads(mine, other, factor, width)).astype(jnp.float16)
     acc = lax.all_to_all(acc.reshape(16, 2 * rows, width), AXES, 0, 0, axis_index_groups=grid)
-    acc = factor * acc.astype(jnp.float32).sum(0)
+    acc = (factor / GRAD_SCALE) * acc.astype(jnp.float32).sum(0)
     both = lax.all_gather(acc, AXES, axis=0, axis_index_groups=pairs).reshape(2, 2, rows, width)
     return tuple(jnp.where(even, side[0], side[1]) for side in both)
 

time: 85.5 us -> 85.4 us (level)
  no operation moved by 1% of the time
where the time goes in v6:
time: 85.4 us; the launch traced here: 85.1 us
  blocking collectives  54.4 us (64%)
  starting transfers between devices  14.3 us (17%)
  waiting for transfers between devices  10 us (12%)
  matrix products  2.31 us (3%)
  Pallas kernels  1.59 us (2%)
  other arithmetic  1.28 us (1%)
    all_to_all x1, blocking collectives, body(): lax.all_to_all(jnp.broadcast_to(mine[None], (16,) + mine.shape), AXES, 0,...  30.7 us
    all_to_all x1, blocking collectives, body(): lax.all_to_all(acc.reshape(16, 2 * rows, width), AXES, 0, 0, axis_index_g...  21.8 us
    all_to_all x1, starting transfers between devices, body(): parts = lax.all_to_all(parts, AXES, 0, 0, axis_index_groups=core_mp)  10.3 us
    all_to_all x1, waiting for transfers between devices, body(): parts = lax.all_to_all(parts, AXES, 0, 0, axis_index_groups=core_mp)  5.49 us
    ppermute x1, waiting for transfers between devices, body(): other = lax.ppermute(mine, AXES, swap)  3.56 us
    dot_general x1, matrix products, body(): lax.dot_general(jnp.stack([spec_feat, pep_feat]), jnp.stack([w_spec, w_pe...  2.31 us
    ppermute x1, starting transfers between devices, body(): got = lax.ppermute(jnp.where(even, t_pep, t_spec), AXES, swap)  2.09 us
    all_gather x1, blocking collectives, body(): lax.all_gather(acc, AXES, axis=0, axis_index_groups=pairs)  1.95 us
  transfers between devices with their start and end apart: 3, of which 3 were waited for; matrix products, arithmetic and copies ran while one was open for 1% of the time, Pallas kernels for 0%

profile of v6, /device:TPU:1, one launch (start us, length us, event | category | flops | bytes accessed | tf_op | source)
XLA Modules:
  0.0 85.1 jit_solution(14797748035877770383)
XLA Ops:
  0.6 0.0 copy-start
  0.6 0.0 copy-start.4
  0.7 0.0 copy-start.1
  0.7 0.0 copy-start.3
  0.7 0.0 copy-start.2
  0.7 2.3 %fusion = f16[2,128,768]{2,1,0:T(8,128)(2,1)} fusion(bf16[1,256,768]{2,1,0:T(8,128)(2,1)} %bitcast.29, bf16[1,256,768]{2,1,0:T(8,128)(2,1)} %bitcast.30, bf16[1,128,256]{2,1,0:T(8,128)(2,1)} %bitcast.31, bf16[1,128,256]{2,1,0:T(8,128)(2,1)} %bitcast.32), kind=kOutput, calls=%fused_computation.3 | convolution fusion | flops 101515264 | bytes 1310720 | tf_op jit(solution)/shard_map/dot_general | solution.py:84
  3.0 10.3 %all-to-all-start = ((f16[16,16,768]{2,1,0:T(8,128)(2,1)}), f16[16,16,768]{2,1,0:T(8,128)(2,1)S(1)}, u32[]{:S(2)}, u32[]{:S(2)}) async-start(f16[16,16,768]{2,1,0:T(8,128)(2,1)} %bitcast.4), calls=%async_computation | async-start | bytes 786432 | tf_op jit(solution)/shard_map/all_to_all | solution.py:91
  13.3 0.0 copy-done.4
  13.3 0.1 convert_bitcast_fusion
  13.4 0.1 copy.12
  13.5 0.1 copy.11
  13.6 0.0 copy-done
  13.6 0.1 pad.10.clone
  13.7 0.0 copy-done.1
  13.7 0.1 broadcast_select_fusion.2
  13.8 2.1 %collective-permute-start = (bf16[16,896]{1,0:T(8,128)(2,1)S(1)}, bf16[16,896]{1,0:T(8,128)(2,1)S(1)}, u32[]{:S(2)}, u32[]{:S(2)}) collective-permute-start(bf16[16,896]{1,0:T(8,128)(2,1)S(1)} %broadcast_select_fusion.2), channel_id=1, source_target_pairs={{0,8},{1,9},{3,11},{2,10},{4,12},{5,13},{7,15},{6,14},{16,24},{17,... | collective-permute-start | bytes 86024 | tf_op jit(solution)/shard_map/ppermute | solution.py:81
  15.9 0.0 copy-done.3
  15.9 0.0 copy-done.2
  15.9 0.9 %collective-permute-done = bf16[16,896]{1,0:T(8,128)(2,1)S(1)} collective-permute-done((bf16[16,896]{1,0:T(8,128)(2,1)S(1)}, bf16[16,896]{1,0:T(8,128)(2,1)S(1)}, u32[]{:S(2)}, u32[]{:S(2)}) %collective-permute-start) | collective-permute-done | bytes 28704 | tf_op jit(solution)/shard_map/ppermute | solution.py:81
  16.9 0.1 broadcast_select_fusion.1
  16.9 5.5 %all-to-all-done = f16[16,16,768]{2,1,0:T(8,128)(2,1)S(1)} async-done(((f16[16,16,768]{2,1,0:T(8,128)(2,1)}), f16[16,16,768]{2,1,0:T(8,128)(2,1)S(1)}, u32[]{:S(2)}, u32[]{:S(2)}) %all-to-all-start) | async-done | bytes 393248 | tf_op jit(solution)/shard_map/all_to_all | solution.py:91
  22.4 0.1 convert_reduce_fusion.1
  22.5 0.1 broadcast_in_dim.20
  22.7 30.7 %all_to_all.15 = bf16[16,32,1664]{2,1,0:T(8,128)(2,1)S(1)} all-to-all(bf16[16,32,1664]{2,1,0:T(8,128)(2,1)S(1)} %broadcast_in_dim.20), channel_id=1, replica_groups={{0,4,128,132,256,260,384,388,3,7,131,135,259,263,387,391},{1,5,129,133,..., dimensions={0} | all-to-all | bytes 3407872 | tf_op jit(solution)/shard_map/all_to_all | solution.py:97
  53.3 1.9 %collective-permute-start.1 = (bf16[512,1664]{1,0:T(8,128)(2,1)S(1)}, bf16[512,1664]{1,0:T(8,128)(2,1)S(1)}, u32[]{:S(2)}, u32[]{:S(2)}) collective-permute-start(bf16[512,1664]{1,0:T(8,128)(2,1)S(1)} %bitcast.25), channel_id=1, source_target_pairs={{0,8},{1,9},{3,11},{2,10},{4,12},{5,13},{7,15},{6,14},{16,24},{17,... | collective-permute-start | bytes 5111816 | tf_op jit(solution)/shard_map/ppermute | solution.py:100
  55.3 3.6 %collective-permute-done.1.refs_1_ = bf16[512,1664]{1,0:T(8,128)(2,1)S(1)} collective-permute-done((bf16[512,1664]{1,0:T(8,128)(2,1)S(1)}, bf16[512,1664]{1,0:T(8,128)(2,1)S(1)}, u32[]{:S(2)}, u32[]{:S(2)}) %collective-permute-start.1) | collective-permute-done | bytes 1703968 | tf_op jit(solution)/shard_map/ppermute | solution.py:100
  58.8 1.6 %shard_map.104 = f32[512,768]{1,0:T(8,128)S(1)} custom-call(bf16[512,1664]{1,0:T(8,128)(2,1)S(1)} %bitcast.26, bf16[512,1664]{1,0:T(8,128)(2,1)S(1)} %collective-permute-done.1.refs_1_), custom_call_target="tpu_custom_call" | custom-call | tf_op jit(solution)/shard_map/pallas_call | solution.py:38
  60.4 0.1 multiply_convert_fusion
  60.6 21.8 %all_to_all.16 = f16[16,32,768]{2,1,0:T(8,128)(2,1)S(1)} all-to-all(f16[16,32,768]{2,1,0:T(8,128)(2,1)S(1)} %bitcast.27), channel_id=1, replica_groups={{0,4,128,132,256,260,384,388,3,7,131,135,259,263,387,391},{1,5,129,133,..., dimensions={0} | all-to-all | bytes 1572864 | tf_op jit(solution)/shard_map/all_to_all | solution.py:103
  82.4 0.1 convert_reduce_fusion
  82.5 1.9 %all-gather = f32[64,768]{1,0:T(8,128)S(1)} all-gather(f32[32,768]{1,0:T(8,128)S(1)} %broadcast_multiply_fusion), channel_id=2, replica_groups={{0,8},{1,9},{3,11},{2,10},{4,12},{5,13},{7,15},{6,14},{16,24},{17,25},{..., dimensions={0}, use_global_device_ids=true | all-gather | bytes 294912 | tf_op jit(solution)/shard_map/all_gather | solution.py:105
  84.4 0.6 fusion.9
  (9 shorter events, 0.1 us)
Async XLA Ops:
  0.6 12.9 %copy-start = (bf16[128,768]{1,0:T(8,128)(2,1)S(1)}, bf16[128,768]{1,0:T(8,128)(2,1)}, u32[]{:S(2)}) copy-start(bf16[128,768]{1,0:T(8,128)(2,1)} %param.13) | copy-start | bytes 589828
  0.6 12.6 %copy-start.4 = (s32[128]{0:T(128)S(1)}, s32[128]{0:T(128)}, u32[]{:S(2)}) copy-start(s32[128]{0:T(128)} %param.17) | copy-start | bytes 1540
  0.7 13.0 %copy-start.1 = (bf16[16,768]{1,0:T(8,128)(2,1)S(1)}, bf16[16,768]{1,0:T(8,128)(2,1)}, u32[]{:S(2)}) copy-start(bf16[16,768]{1,0:T(8,128)(2,1)} %param.14) | copy-start | bytes 73732
  0.7 15.2 %copy-start.3 = (s32[768]{0:T(1024)S(1)}, s32[768]{0:T(1024)}, u32[]{:S(2)}) copy-start(s32[768]{0:T(1024)} %param.16) | copy-start | bytes 9220
  0.7 15.2 %copy-start.2 = (s32[768]{0:T(1024)S(1)}, s32[768]{0:T(1024)}, u32[]{:S(2)}) copy-start(s32[768]{0:T(1024)} %param.15) | copy-start | bytes 9220
  3.0 19.4 %all-to-all-start = ((f16[16,16,768]{2,1,0:T(8,128)(2,1)}), f16[16,16,768]{2,1,0:T(8,128)(2,1)S(1)}, u32[]{:S(2)}, u32[]{:S(2)}) async-start(f16[16,16,768]{2,1,0:T(8,128)(2,1)} %bitcast.4), calls=%async_computation | async-start | bytes 786432 | tf_op jit(solution)/shard_map/all_to_all | solution.py:91
  13.8 3.1 %collective-permute-start = (bf16[16,896]{1,0:T(8,128)(2,1)S(1)}, bf16[16,896]{1,0:T(8,128)(2,1)S(1)}, u32[]{:S(2)}, u32[]{:S(2)}) collective-permute-start(bf16[16,896]{1,0:T(8,128)(2,1)S(1)} %broadcast_select_fusion.2), channel_id=1, source_target_pairs={{0,8},{1,9},{3,11},{2,10},{4,12},{5,13},{7,15},{6,14},{16,24},{17,... | collective-permute-start | bytes 86024 | tf_op jit(solution)/shard_map/ppermute | solution.py:81
  53.3 5.5 %collective-permute-start.1 = (bf16[512,1664]{1,0:T(8,128)(2,1)S(1)}, bf16[512,1664]{1,0:T(8,128)(2,1)S(1)}, u32[]{:S(2)}, u32[]{:S(2)}) collective-permute-start(bf16[512,1664]{1,0:T(8,128)(2,1)S(1)} %bitcast.25), channel_id=1, source_target_pairs={{0,8},{1,9},{3,11},{2,10},{4,12},{5,13},{7,15},{6,14},{16,24},{17,... | collective-permute-start | bytes 5111816 | tf_op jit(solution)/shard_map/ppermute | solution.py:100

commit v7 on v6

--- a/solution.py
+++ b/solution.py
@@ -50,8 +50,8 @@
     flat = flat[..., [0, 1, 3, 2]].reshape(4, 8, 2, 2, 2, 2)
     even = flat[:, :, 0]
     odd = flat[:, :, 1]
-    spec_side = even.transpose(1, 4, 3, 0, 2).reshape(16, 16)
-    pep_side = odd.transpose(0, 2, 3, 4, 1).reshape(16, 16)
+    spec_side = even.transpose(0, 2, 4, 3, 1).reshape(16, 16)
+    pep_side = odd.transpose(1, 3, 4, 0, 2).reshape(16, 16)
     grid = np.concatenate([spec_side, pep_side], 0)
     pairs = [(int(a), int(b)) for a, b in zip(flat[:, :, 0].ravel(), flat[:, :, 1].ravel())]
     swap = pairs + [(b, a) for a, b in pairs]
@@ -102,8 +102,10 @@
     acc = (GRAD_SCALE * pair_grads(mine, other, factor, width)).astype(jnp.float16)
     acc = lax.all_to_all(acc.reshape(16, 2 * rows, width), AXES, 0, 0, axis_index_groups=grid)
     acc = (factor / GRAD_SCALE) * acc.astype(jnp.float32).sum(0)
-    both = lax.all_gather(acc, AXES, axis=0, axis_index_groups=pairs).reshape(2, 2, rows, width)
-    return tuple(jnp.where(even, side[0], side[1]) for side in both)
+    own, foreign = jnp.where(even, acc[:rows], acc[rows:]), jnp.where(even, acc[rows:], acc[:rows])
+    both = lax.all_gather(foreign, AXES, axis=0, axis_index_groups=pairs)
+    got = jnp.where(even, both[1], both[0])
+    return jnp.where(even, own, got), jnp.where(even, got, own)
 
 
 def solution(mesh):

time: 85.4 us -> 85.4 us (level)
  starting transfers between devices: 14.3 us -> 21.2 us
  blocking collectives: 54.4 us -> 47.8 us
    ppermute x1, starting transfers between devices: 1.91 us -> 8.87 us  [body(): other = lax.ppermute(mine, AXES, swap)]
    all_to_all x1, blocking collectives: 30.7 us -> 26.8 us  [body(): lax.all_to_all(jnp.broadcast_to(mine[None], (16,) + mine.shape), AXES, 0,...]
    all_to_all x1, blocking collectives: 21.8 us -> 19.1 us  [body(): lax.all_to_all(acc.reshape(16, 2 * rows, width), AXES, 0, 0, axis_index_g...]
where the time goes in v7:
time: 85.4 us; the launch traced here: 85 us
  blocking collectives  47.8 us (56%)
  starting transfers between devices  21.2 us (25%)
  waiting for transfers between devices  9.64 us (11%)
  matrix products  2.31 us (3%)
  Pallas kernels  1.6 us (2%)
  other arithmetic  1.3 us (2%)
    all_to_all x1, blocking collectives, body(): lax.all_to_all(jnp.broadcast_to(mine[None], (16,) + mine.shape), AXES, 0,...  26.8 us
    all_to_all x1, blocking collectives, body(): lax.all_to_all(acc.reshape(16, 2 * rows, width), AXES, 0, 0, axis_index_g...  19.1 us
    all_to_all x1, starting transfers between devices, body(): parts = lax.all_to_all(parts, AXES, 0, 0, axis_index_groups=core_mp)  10.3 us
    ppermute x1, starting transfers between devices, body(): other = lax.ppermute(mine, AXES, swap)  8.87 us
    all_to_all x1, waiting for transfers between devices, body(): parts = lax.all_to_all(parts, AXES, 0, 0, axis_index_groups=core_mp)  5.49 us
    ppermute x1, waiting for transfers between devices, body(): other = lax.ppermute(mine, AXES, swap)  3.2 us
    dot_general x1, matrix products, body(): lax.dot_general(jnp.stack([spec_feat, pep_feat]), jnp.stack([w_spec, w_pe...  2.31 us
    ppermute x1, starting transfers between devices, body(): got = lax.ppermute(jnp.where(even, t_pep, t_spec), AXES, swap)  2.09 us
  transfers between devices with their start and end apart: 3, of which 3 were waited for; matrix products, arithmetic and copies ran while one was open for 1% of the time, Pallas kernels for 0%

profile of v7, /device:TPU:1, one launch (start us, length us, event | category | flops | bytes accessed | tf_op | source)
XLA Modules:
  0.0 85.0 jit_solution(15569751407150163932)
XLA Ops:
  0.6 0.0 copy-start
  0.6 0.0 copy-start.4
  0.7 0.0 copy-start.1
  0.7 0.0 copy-start.3
  0.7 0.0 copy-start.2
  0.7 2.3 %fusion = f16[2,128,768]{2,1,0:T(8,128)(2,1)} fusion(bf16[1,256,768]{2,1,0:T(8,128)(2,1)} %bitcast.23, bf16[1,256,768]{2,1,0:T(8,128)(2,1)} %bitcast.24, bf16[1,128,256]{2,1,0:T(8,128)(2,1)} %bitcast.25, bf16[1,128,256]{2,1,0:T(8,128)(2,1)} %bitcast.26), kind=kOutput, calls=%fused_computation.3 | convolution fusion | flops 101515264 | bytes 1310720 | tf_op jit(solution)/shard_map/dot_general | solution.py:84
  3.0 10.3 %all-to-all-start = ((f16[16,16,768]{2,1,0:T(8,128)(2,1)}), f16[16,16,768]{2,1,0:T(8,128)(2,1)S(1)}, u32[]{:S(2)}, u32[]{:S(2)}) async-start(f16[16,16,768]{2,1,0:T(8,128)(2,1)} %bitcast.4), calls=%async_computation | async-start | bytes 786432 | tf_op jit(solution)/shard_map/all_to_all | solution.py:91
  13.3 0.0 copy-done.4
  13.3 0.1 convert_bitcast_fusion
  13.4 0.1 copy.12
  13.5 0.1 copy.11
  13.6 0.0 copy-done
  13.6 0.1 pad.10.clone
  13.7 0.0 copy-done.1
  13.7 0.1 broadcast_select_fusion.2
  13.8 2.1 %collective-permute-start = (bf16[16,896]{1,0:T(8,128)(2,1)S(1)}, bf16[16,896]{1,0:T(8,128)(2,1)S(1)}, u32[]{:S(2)}, u32[]{:S(2)}) collective-permute-start(bf16[16,896]{1,0:T(8,128)(2,1)S(1)} %broadcast_select_fusion.2), channel_id=1, source_target_pairs={{0,8},{1,9},{3,11},{2,10},{4,12},{5,13},{7,15},{6,14},{16,24},{17,... | collective-permute-start | bytes 86024 | tf_op jit(solution)/shard_map/ppermute | solution.py:81
  15.9 0.0 copy-done.3
  15.9 0.0 copy-done.2
  15.9 0.9 %collective-permute-done = bf16[16,896]{1,0:T(8,128)(2,1)S(1)} collective-permute-done((bf16[16,896]{1,0:T(8,128)(2,1)S(1)}, bf16[16,896]{1,0:T(8,128)(2,1)S(1)}, u32[]{:S(2)}, u32[]{:S(2)}) %collective-permute-start) | collective-permute-done | bytes 28704 | tf_op jit(solution)/shard_map/ppermute | solution.py:81
  16.9 0.1 broadcast_select_fusion.1
  16.9 5.5 %all-to-all-done = f16[16,16,768]{2,1,0:T(8,128)(2,1)S(1)} async-done(((f16[16,16,768]{2,1,0:T(8,128)(2,1)}), f16[16,16,768]{2,1,0:T(8,128)(2,1)S(1)}, u32[]{:S(2)}, u32[]{:S(2)}) %all-to-all-start) | async-done | bytes 393248 | tf_op jit(solution)/shard_map/all_to_all | solution.py:91
  22.4 0.1 convert_reduce_fusion.1
  22.5 0.1 broadcast_in_dim.20
  22.7 26.8 %all_to_all.15 = bf16[16,32,1664]{2,1,0:T(8,128)(2,1)S(1)} all-to-all(bf16[16,32,1664]{2,1,0:T(8,128)(2,1)S(1)} %broadcast_in_dim.20), channel_id=1, replica_groups={{0,16,32,48,64,80,96,112,3,19,35,51,67,83,99,115},{1,17,33,49,65,81,97,..., dimensions={0} | all-to-all | bytes 3407872 | tf_op jit(solution)/shard_map/all_to_all | solution.py:97
  49.4 8.9 %collective-permute-start.1 = (bf16[512,1664]{1,0:T(8,128)(2,1)S(1)}, bf16[512,1664]{1,0:T(8,128)(2,1)S(1)}, u32[]{:S(2)}, u32[]{:S(2)}) collective-permute-start(bf16[512,1664]{1,0:T(8,128)(2,1)S(1)} %bitcast.20), channel_id=1, source_target_pairs={{0,8},{1,9},{3,11},{2,10},{4,12},{5,13},{7,15},{6,14},{16,24},{17,... | collective-permute-start | bytes 5111816 | tf_op jit(solution)/shard_map/ppermute | solution.py:100
  58.3 3.2 %collective-permute-done.1.refs_1_ = bf16[512,1664]{1,0:T(8,128)(2,1)S(1)} collective-permute-done((bf16[512,1664]{1,0:T(8,128)(2,1)S(1)}, bf16[512,1664]{1,0:T(8,128)(2,1)S(1)}, u32[]{:S(2)}, u32[]{:S(2)}) %collective-permute-start.1) | collective-permute-done | bytes 1703968 | tf_op jit(solution)/shard_map/ppermute | solution.py:100
  61.5 1.6 %shard_map.104 = f32[512,768]{1,0:T(8,128)S(1)} custom-call(bf16[512,1664]{1,0:T(8,128)(2,1)S(1)} %bitcast.21, bf16[512,1664]{1,0:T(8,128)(2,1)S(1)} %collective-permute-done.1.refs_1_), custom_call_target="tpu_custom_call" | custom-call | tf_op jit(solution)/shard_map/pallas_call | solution.py:38
  63.1 0.1 multiply_convert_fusion
  63.3 19.1 %all_to_all.16 = f16[16,32,768]{2,1,0:T(8,128)(2,1)S(1)} all-to-all(f16[16,32,768]{2,1,0:T(8,128)(2,1)S(1)} %bitcast.22), channel_id=1, replica_groups={{0,16,32,48,64,80,96,112,3,19,35,51,67,83,99,115},{1,17,33,49,65,81,97,..., dimensions={0} | all-to-all | bytes 1572864 | tf_op jit(solution)/shard_map/all_to_all | solution.py:103
  82.4 0.1 convert_reduce_fusion
  82.5 1.9 %all-gather = f32[32,768]{1,0:T(8,128)S(1)} all-gather(f32[16,768]{1,0:T(8,128)S(1)} %slice_select_fusion.1), channel_id=2, replica_groups={{0,8},{1,9},{3,11},{2,10},{4,12},{5,13},{7,15},{6,14},{16,24},{17,25},{..., dimensions={0}, use_global_device_ids=true | all-gather | bytes 147456 | tf_op jit(solution)/shard_map/all_gather | solution.py:106
  84.4 0.7 broadcast_select_fusion.4
  (10 shorter events, 0.1 us)
Async XLA Ops:
  0.6 12.9 %copy-start = (bf16[128,768]{1,0:T(8,128)(2,1)S(1)}, bf16[128,768]{1,0:T(8,128)(2,1)}, u32[]{:S(2)}) copy-start(bf16[128,768]{1,0:T(8,128)(2,1)} %param.13) | copy-start | bytes 589828
  0.6 12.6 %copy-start.4 = (s32[128]{0:T(128)S(1)}, s32[128]{0:T(128)}, u32[]{:S(2)}) copy-start(s32[128]{0:T(128)} %param.17) | copy-start | bytes 1540
  0.7 13.0 %copy-start.1 = (bf16[16,768]{1,0:T(8,128)(2,1)S(1)}, bf16[16,768]{1,0:T(8,128)(2,1)}, u32[]{:S(2)}) copy-start(bf16[16,768]{1,0:T(8,128)(2,1)} %param.14) | copy-start | bytes 73732
  0.7 15.2 %copy-start.3 = (s32[768]{0:T(1024)S(1)}, s32[768]{0:T(1024)}, u32[]{:S(2)}) copy-start(s32[768]{0:T(1024)} %param.16) | copy-start | bytes 9220
  0.7 15.2 %copy-start.2 = (s32[768]{0:T(1024)S(1)}, s32[768]{0:T(1024)}, u32[]{:S(2)}) copy-start(s32[768]{0:T(1024)} %param.15) | copy-start | bytes 9220
  3.0 19.4 %all-to-all-start = ((f16[16,16,768]{2,1,0:T(8,128)(2,1)}), f16[16,16,768]{2,1,0:T(8,128)(2,1)S(1)}, u32[]{:S(2)}, u32[]{:S(2)}) async-start(f16[16,16,768]{2,1,0:T(8,128)(2,1)} %bitcast.4), calls=%async_computation | async-start | bytes 786432 | tf_op jit(solution)/shard_map/all_to_all | solution.py:91
  13.8 3.1 %collective-permute-start = (bf16[16,896]{1,0:T(8,128)(2,1)S(1)}, bf16[16,896]{1,0:T(8,128)(2,1)S(1)}, u32[]{:S(2)}, u32[]{:S(2)}) collective-permute-start(bf16[16,896]{1,0:T(8,128)(2,1)S(1)} %broadcast_select_fusion.2), channel_id=1, source_target_pairs={{0,8},{1,9},{3,11},{2,10},{4,12},{5,13},{7,15},{6,14},{16,24},{17,... | collective-permute-start | bytes 86024 | tf_op jit(solution)/shard_map/ppermute | solution.py:81
  49.4 12.1 %collective-permute-start.1 = (bf16[512,1664]{1,0:T(8,128)(2,1)S(1)}, bf16[512,1664]{1,0:T(8,128)(2,1)S(1)}, u32[]{:S(2)}, u32[]{:S(2)}) collective-permute-start(bf16[512,1664]{1,0:T(8,128)(2,1)S(1)} %bitcast.20), channel_id=1, source_target_pairs={{0,8},{1,9},{3,11},{2,10},{4,12},{5,13},{7,15},{6,14},{16,24},{17,... | collective-permute-start | bytes 5111816 | tf_op jit(solution)/shard_map/ppermute | solution.py:100

commit v8 on v7

--- a/solution.py
+++ b/solution.py
@@ -31,7 +31,7 @@
     target = 0.25 * jnp.tanh((0.5 * factor) * teacher) - 0.25 + hard
     student = lax.dot_general(mine[:, :width], other[:, :width], inner, preferred_element_type=jnp.float32)
     grads = 0.5 * jnp.tanh((0.5 * factor) * student + 0.5 * LOGIT_SHIFT) - target
-    out[...] = jnp.dot(grads.astype(jnp.bfloat16), other[:, :width], preferred_element_type=jnp.float32)
+    out[...] = GRAD_SCALE * jnp.dot(grads.astype(jnp.bfloat16), other[:, :width], preferred_element_type=jnp.float32)
 
 
 def pair_grads(mine, other, factor, width):
@@ -50,8 +50,8 @@
     flat = flat[..., [0, 1, 3, 2]].reshape(4, 8, 2, 2, 2, 2)
     even = flat[:, :, 0]
     odd = flat[:, :, 1]
-    spec_side = even.transpose(0, 2, 4, 3, 1).reshape(16, 16)
-    pep_side = odd.transpose(1, 3, 4, 0, 2).reshape(16, 16)
+    spec_side = even.transpose(1, 4, 3, 0, 2).reshape(16, 16)
+    pep_side = odd.transpose(0, 2, 3, 4, 1).reshape(16, 16)
     grid = np.concatenate([spec_side, pep_side], 0)
     pairs = [(int(a), int(b)) for a, b in zip(flat[:, :, 0].ravel(), flat[:, :, 1].ravel())]
     swap = pairs + [(b, a) for a, b in pairs]
@@ -99,7 +99,7 @@
     ).reshape(16 * 2 * rows, -1)
     other = lax.ppermute(mine, AXES, swap)
 
-    acc = (GRAD_SCALE * pair_grads(mine, other, factor, width)).astype(jnp.float16)
+    acc = pair_grads(mine, other, factor, width).astype(jnp.float16)
     acc = lax.all_to_all(acc.reshape(16, 2 * rows, width), AXES, 0, 0, axis_index_groups=grid)
     acc = (factor / GRAD_SCALE) * acc.astype(jnp.float32).sum(0)
     own, foreign = jnp.where(even, acc[:rows], acc[rows:]), jnp.where(even, acc[rows:], acc[:rows])

time: 85.4 us -> 85.3 us (level)
  starting transfers between devices: 21.2 us -> 14.3 us
  blocking collectives: 47.8 us -> 54.4 us
    ppermute x1, starting transfers between devices: 8.87 us -> 1.91 us  [body(): other = lax.ppermute(mine, AXES, swap)]
    all_to_all x1, blocking collectives: 26.8 us -> 30.7 us  [body(): lax.all_to_all(jnp.broadcast_to(mine[None], (16,) + mine.shape), AXES, 0,...]
    all_to_all x1, blocking collectives: 19.1 us -> 21.8 us  [body(): lax.all_to_all(acc.reshape(16, 2 * rows, width), AXES, 0, 0, axis_index_g...]
where the time goes in v8:
time: 85.3 us; the launch traced here: 85 us
  blocking collectives  54.4 us (64%)
  starting transfers between devices  14.3 us (17%)
  waiting for transfers between devices  10 us (12%)
  matrix products  2.31 us (3%)
  Pallas kernels  1.59 us (2%)
  other arithmetic  1.25 us (1%)
    all_to_all x1, blocking collectives, body(): lax.all_to_all(jnp.broadcast_to(mine[None], (16,) + mine.shape), AXES, 0,...  30.7 us
    all_to_all x1, blocking collectives, body(): lax.all_to_all(acc.reshape(16, 2 * rows, width), AXES, 0, 0, axis_index_g...  21.8 us
    all_to_all x1, starting transfers between devices, body(): parts = lax.all_to_all(parts, AXES, 0, 0, axis_index_groups=core_mp)  10.3 us
    all_to_all x1, waiting for transfers between devices, body(): parts = lax.all_to_all(parts, AXES, 0, 0, axis_index_groups=core_mp)  5.49 us
    ppermute x1, waiting for transfers between devices, body(): other = lax.ppermute(mine, AXES, swap)  3.56 us
    dot_general x1, matrix products, body(): lax.dot_general(jnp.stack([spec_feat, pep_feat]), jnp.stack([w_spec, w_pe...  2.31 us
    ppermute x1, starting transfers between devices, body(): got = lax.ppermute(jnp.where(even, t_pep, t_spec), AXES, swap)  2.09 us
    ppermute x1, starting transfers between devices, body(): other = lax.ppermute(mine, AXES, swap)  1.91 us
  transfers between devices with their start and end apart: 3, of which 3 were waited for; matrix products, arithmetic and copies ran while one was open for 1% of the time, Pallas kernels for 0%

profile of v8, /device:TPU:1, one launch (start us, length us, event | category | flops | bytes accessed | tf_op | source)
XLA Modules:
  0.0 85.0 jit_solution(8343236143753006454)
XLA Ops:
  0.6 0.0 copy-start
  0.6 0.0 copy-start.4
  0.7 0.0 copy-start.1
  0.7 0.0 copy-start.3
  0.7 0.0 copy-start.2
  0.7 2.3 %fusion = f16[2,128,768]{2,1,0:T(8,128)(2,1)} fusion(bf16[1,256,768]{2,1,0:T(8,128)(2,1)} %bitcast.23, bf16[1,256,768]{2,1,0:T(8,128)(2,1)} %bitcast.24, bf16[1,128,256]{2,1,0:T(8,128)(2,1)} %bitcast.25, bf16[1,128,256]{2,1,0:T(8,128)(2,1)} %bitcast.26), kind=kOutput, calls=%fused_computation.2 | convolution fusion | flops 101515264 | bytes 1310720 | tf_op jit(solution)/shard_map/dot_general | solution.py:84
  3.0 10.3 %all-to-all-start = ((f16[16,16,768]{2,1,0:T(8,128)(2,1)}), f16[16,16,768]{2,1,0:T(8,128)(2,1)S(1)}, u32[]{:S(2)}, u32[]{:S(2)}) async-start(f16[16,16,768]{2,1,0:T(8,128)(2,1)} %bitcast.4), calls=%async_computation | async-start | bytes 786432 | tf_op jit(solution)/shard_map/all_to_all | solution.py:91
  13.3 0.0 copy-done.4
  13.3 0.1 convert_bitcast_fusion
  13.4 0.1 copy.12
  13.5 0.1 copy.11
  13.6 0.0 copy-done
  13.6 0.1 pad.10.clone
  13.7 0.0 copy-done.1
  13.7 0.1 broadcast_select_fusion.2
  13.8 2.1 %collective-permute-start = (bf16[16,896]{1,0:T(8,128)(2,1)S(1)}, bf16[16,896]{1,0:T(8,128)(2,1)S(1)}, u32[]{:S(2)}, u32[]{:S(2)}) collective-permute-start(bf16[16,896]{1,0:T(8,128)(2,1)S(1)} %broadcast_select_fusion.2), channel_id=1, source_target_pairs={{0,8},{1,9},{3,11},{2,10},{4,12},{5,13},{7,15},{6,14},{16,24},{17,... | collective-permute-start | bytes 86024 | tf_op jit(solution)/shard_map/ppermute | solution.py:81
  15.9 0.0 copy-done.3
  15.9 0.0 copy-done.2
  15.9 0.9 %collective-permute-done = bf16[16,896]{1,0:T(8,128)(2,1)S(1)} collective-permute-done((bf16[16,896]{1,0:T(8,128)(2,1)S(1)}, bf16[16,896]{1,0:T(8,128)(2,1)S(1)}, u32[]{:S(2)}, u32[]{:S(2)}) %collective-permute-start) | collective-permute-done | bytes 28704 | tf_op jit(solution)/shard_map/ppermute | solution.py:81
  16.9 0.1 broadcast_select_fusion.1
  16.9 5.5 %all-to-all-done = f16[16,16,768]{2,1,0:T(8,128)(2,1)S(1)} async-done(((f16[16,16,768]{2,1,0:T(8,128)(2,1)}), f16[16,16,768]{2,1,0:T(8,128)(2,1)S(1)}, u32[]{:S(2)}, u32[]{:S(2)}) %all-to-all-start) | async-done | bytes 393248 | tf_op jit(solution)/shard_map/all_to_all | solution.py:91
  22.4 0.1 convert_reduce_fusion.1
  22.5 0.1 broadcast_in_dim.20
  22.7 30.7 %all_to_all.15 = bf16[16,32,1664]{2,1,0:T(8,128)(2,1)S(1)} all-to-all(bf16[16,32,1664]{2,1,0:T(8,128)(2,1)S(1)} %broadcast_in_dim.20), channel_id=1, replica_groups={{0,4,128,132,256,260,384,388,3,7,131,135,259,263,387,391},{1,5,129,133,..., dimensions={0} | all-to-all | bytes 3407872 | tf_op jit(solution)/shard_map/all_to_all | solution.py:97
  53.3 1.9 %collective-permute-start.1 = (bf16[512,1664]{1,0:T(8,128)(2,1)S(1)}, bf16[512,1664]{1,0:T(8,128)(2,1)S(1)}, u32[]{:S(2)}, u32[]{:S(2)}) collective-permute-start(bf16[512,1664]{1,0:T(8,128)(2,1)S(1)} %bitcast.20), channel_id=1, source_target_pairs={{0,8},{1,9},{3,11},{2,10},{4,12},{5,13},{7,15},{6,14},{16,24},{17,... | collective-permute-start | bytes 5111816 | tf_op jit(solution)/shard_map/ppermute | solution.py:100
  55.3 3.6 %collective-permute-done.1.refs_1_ = bf16[512,1664]{1,0:T(8,128)(2,1)S(1)} collective-permute-done((bf16[512,1664]{1,0:T(8,128)(2,1)S(1)}, bf16[512,1664]{1,0:T(8,128)(2,1)S(1)}, u32[]{:S(2)}, u32[]{:S(2)}) %collective-permute-start.1) | collective-permute-done | bytes 1703968 | tf_op jit(solution)/shard_map/ppermute | solution.py:100
  58.8 1.6 %shard_map.104 = f32[512,768]{1,0:T(8,128)S(1)} custom-call(bf16[512,1664]{1,0:T(8,128)(2,1)S(1)} %bitcast.21, bf16[512,1664]{1,0:T(8,128)(2,1)S(1)} %collective-permute-done.1.refs_1_), custom_call_target="tpu_custom_call" | custom-call | tf_op jit(solution)/shard_map/pallas_call | solution.py:38
  60.4 0.1 convert_element_type.56
  60.5 21.8 %all_to_all.16 = f16[16,32,768]{2,1,0:T(8,128)(2,1)S(1)} all-to-all(f16[16,32,768]{2,1,0:T(8,128)(2,1)S(1)} %bitcast.22), channel_id=1, replica_groups={{0,4,128,132,256,260,384,388,3,7,131,135,259,263,387,391},{1,5,129,133,..., dimensions={0} | all-to-all | bytes 1572864 | tf_op jit(solution)/shard_map/all_to_all | solution.py:103
  82.3 0.1 convert_reduce_fusion
  82.5 1.9 %all-gather = f32[32,768]{1,0:T(8,128)S(1)} all-gather(f32[16,768]{1,0:T(8,128)S(1)} %slice_select_fusion.1), channel_id=2, replica_groups={{0,8},{1,9},{3,11},{2,10},{4,12},{5,13},{7,15},{6,14},{16,24},{17,25},{..., dimensions={0}, use_global_device_ids=true | all-gather | bytes 147456 | tf_op jit(solution)/shard_map/all_gather | solution.py:106
  84.3 0.7 broadcast_select_fusion.4
  (10 shorter events, 0.1 us)
Async XLA Ops:
  0.6 12.9 %copy-start = (bf16[128,768]{1,0:T(8,128)(2,1)S(1)}, bf16[128,768]{1,0:T(8,128)(2,1)}, u32[]{:S(2)}) copy-start(bf16[128,768]{1,0:T(8,128)(2,1)} %param.13) | copy-start | bytes 589828
  0.6 12.6 %copy-start.4 = (s32[128]{0:T(128)S(1)}, s32[128]{0:T(128)}, u32[]{:S(2)}) copy-start(s32[128]{0:T(128)} %param.17) | copy-start | bytes 1540
  0.7 13.0 %copy-start.1 = (bf16[16,768]{1,0:T(8,128)(2,1)S(1)}, bf16[16,768]{1,0:T(8,128)(2,1)}, u32[]{:S(2)}) copy-start(bf16[16,768]{1,0:T(8,128)(2,1)} %param.14) | copy-start | bytes 73732
  0.7 15.2 %copy-start.3 = (s32[768]{0:T(1024)S(1)}, s32[768]{0:T(1024)}, u32[]{:S(2)}) copy-start(s32[768]{0:T(1024)} %param.16) | copy-start | bytes 9220
  0.7 15.2 %copy-start.2 = (s32[768]{0:T(1024)S(1)}, s32[768]{0:T(1024)}, u32[]{:S(2)}) copy-start(s32[768]{0:T(1024)} %param.15) | copy-start | bytes 9220
  3.0 19.4 %all-to-all-start = ((f16[16,16,768]{2,1,0:T(8,128)(2,1)}), f16[16,16,768]{2,1,0:T(8,128)(2,1)S(1)}, u32[]{:S(2)}, u32[]{:S(2)}) async-start(f16[16,16,768]{2,1,0:T(8,128)(2,1)} %bitcast.4), calls=%async_computation | async-start | bytes 786432 | tf_op jit(solution)/shard_map/all_to_all | solution.py:91
  13.8 3.1 %collective-permute-start = (bf16[16,896]{1,0:T(8,128)(2,1)S(1)}, bf16[16,896]{1,0:T(8,128)(2,1)S(1)}, u32[]{:S(2)}, u32[]{:S(2)}) collective-permute-start(bf16[16,896]{1,0:T(8,128)(2,1)S(1)} %broadcast_select_fusion.2), channel_id=1, source_target_pairs={{0,8},{1,9},{3,11},{2,10},{4,12},{5,13},{7,15},{6,14},{16,24},{17,... | collective-permute-start | bytes 86024 | tf_op jit(solution)/shard_map/ppermute | solution.py:81
  53.3 5.5 %collective-permute-start.1 = (bf16[512,1664]{1,0:T(8,128)(2,1)S(1)}, bf16[512,1664]{1,0:T(8,128)(2,1)S(1)}, u32[]{:S(2)}, u32[]{:S(2)}) collective-permute-start(bf16[512,1664]{1,0:T(8,128)(2,1)S(1)} %bitcast.20), channel_id=1, source_target_pairs={{0,8},{1,9},{3,11},{2,10},{4,12},{5,13},{7,15},{6,14},{16,24},{17,... | collective-permute-start | bytes 5111816 | tf_op jit(solution)/shard_map/ppermute | solution.py:100
